TPU v7x, 32 devices: a whole 2x2x4 slice. The times are simulated.
32 devices in a mesh: seq: 8 (over z, x), crop: 4 (over y, core).
Axes of the slice: x: 2, y: 2, z: 4, core: 2. Of those that a mesh axis runs over, the one named last changes fastest.
Arguments:
- pair_state: bfloat16 [8, 256, 256, 128], P('crop', 'seq'), may hold values from -6 to 6
- crop_lengths: int32 [4, 2], P('crop'), may hold values from 64 to 256, as said below
- norm_gain: float32 [2, 3, 128], replicated, may hold values from 0.5 to 1.5
- norm_shift: float32 [2, 3, 128], replicated, may hold values from -1.5 to 1.5
- attend_weight: bfloat16 [2, 2, 128, 512], replicated, may hold values from -0.5 to 0.5
- gate_bias: float32 [2, 2, 128], replicated, may hold values from -4 to 4
- attend_output: bfloat16 [2, 2, 128, 128], replicated, may hold values from -4 to 4
- output_bias: float32 [2, 2, 128], replicated, may hold values from -1.5 to 1.5
- expand_weight: bfloat16 [2, 128, 512], replicated, may hold values from -0.5 to 0.5
- expand_bias: float32 [2, 512], replicated, may hold values from -2.5 to 2.5
- contract_weight: bfloat16 [2, 512, 128], replicated, may hold values from -0.5 to 0.5
- contract_bias: float32 [2, 128], replicated, may hold values from -1.5 to 1.5
- cotangent: bfloat16 [8, 256, 256, 128], P('crop', 'seq'), may hold values from -6 to 6
Outputs:
- pair_output: bfloat16 [8, 256, 256, 128], P('crop', 'seq')
- pair_grad: float32 [8, 256, 256, 128], P('crop', 'seq')
- grad_norm_gain: float32 [2, 3, 128], replicated
- grad_norm_shift: float32 [2, 3, 128], replicated
- grad_attend_weight: float32 [2, 2, 128, 512], replicated
- grad_gate_bias: float32 [2, 2, 128], replicated
- grad_attend_output: float32 [2, 2, 128, 128], replicated
- grad_output_bias: float32 [2, 2, 128], replicated
- grad_expand_weight: float32 [2, 128, 512], replicated
- grad_expand_bias: float32 [2, 512], replicated
- grad_contract_weight: float32 [2, 512, 128], replicated
- grad_contract_bias: float32 [2, 128], replicated
Inputs may be any that keep to these rules, and one draw needn't show every extreme that they name: `crop_lengths`: each row holds the lengths of the 2 crops of one group; one of them, at a place that varies from group to group, equals 256, and the others lie between 64 and 256.
All inputs are finite; a program needn't handle non-finite values.
Results may differ from a plain program's by a relative error of at most 0.019.
Values may be sent and summed in bfloat16 or wider, within the bound.
No kernel may reach another device: no remote copies, remote signals or barrier semaphores. Data moves between devices by JAX's collectives and lax.ppermute only.
A program may use at most 768 MiB of HBM per device.

v0:
```python
import jax
import jax.numpy as jnp
from jax import lax
from jax.sharding import PartitionSpec as P

HEADS = 4
LAYERS = 2


neg_big = -1000000000.0
gelu_coeff = 0.7978845608028654


def layer_norm(x, scale_row, offset_row):
    average = jnp.mean(x, axis=-1, keepdims=True)
    centred = x - average
    variance = jnp.mean(centred * centred, axis=-1, keepdims=True)
    return centred * lax.rsqrt(variance + 1e-05) * scale_row + offset_row


def smooth_gate(t):
    return 0.5 * t * (1.0 + jnp.tanh(gelu_coeff * (t + 0.044715 * t * t * t)))


def score_specs(column):
    if column:
        return ("qxhd,kxhd->xhqk", "xhqk,kxhd->qxhd", "xhqk,qxhd->kxhd")
    return ("xqhd,xkhd->xhqk", "xhqk,xkhd->xqhd", "xhqk,xqhd->xkhd")


def split_heads(t):
    return t.reshape(t.shape[:-1] + (HEADS, t.shape[-1] // HEADS))


def merge_heads(t):
    return t.reshape(t.shape[:-2] + (t.shape[-2] * t.shape[-1],))


def attend_forward(a, weight_in, gate_shift, weight_out, key_shift, column):
    model_width = weight_out.shape[0]
    score_scale = (model_width // HEADS) ** (-0.5)
    h = jnp.einsum("bxyc,cf->bxyf", a, weight_in, preferred_element_type=jnp.float32)
    queries = split_heads(h[..., :model_width].astype(jnp.bfloat16))
    keys_all = split_heads(h[..., model_width : 2 * model_width].astype(jnp.bfloat16))
    values = split_heads(h[..., 2 * model_width : 3 * model_width].astype(jnp.bfloat16))
    gates = jax.nn.sigmoid(h[..., 3 * model_width :] + gate_shift)
    score_spec, output_spec, _ = score_specs(column)

    def one_crop(pieces):
        q, k, v, shift_row = pieces
        scores = (
            jnp.einsum(score_spec, q, k, preferred_element_type=jnp.float32) * score_scale
            + shift_row
        )
        highest = jnp.max(scores, axis=-1, keepdims=True)
        powers = jnp.exp(scores - highest)
        softmax_total = jnp.sum(powers, axis=-1, keepdims=True)
        probability = (powers / softmax_total).astype(jnp.bfloat16)
        attended = jnp.einsum(output_spec, probability, v, preferred_element_type=jnp.float32)
        return (attended, highest + jnp.log(softmax_total))

    attended, log_total = lax.map(one_crop, (queries, keys_all, values, key_shift))
    attended = merge_heads(attended)
    mixed = (attended * gates).astype(jnp.bfloat16)
    branch = jnp.einsum("bxyc,cf->bxyf", mixed, weight_out, preferred_element_type=jnp.float32)
    return (branch, (queries, keys_all, values, gates, attended, log_total))


def attend_backward(a, weight_in, weight_out, key_shift, saved, back_branch, column):
    queries, keys_all, values, gates, attended, log_total = saved
    model_width = weight_out.shape[0]
    score_scale = (model_width // HEADS) ** (-0.5)
    mixed = (attended * gates).astype(jnp.bfloat16)
    back_out_w = jnp.einsum("bxyc,bxyf->cf", mixed, back_branch, preferred_element_type=jnp.float32)
    back_mixed = jnp.einsum(
        "bxyf,cf->bxyc", back_branch, weight_out, preferred_element_type=jnp.float32
    )
    back_attended = split_heads((back_mixed * gates).astype(jnp.bfloat16))
    back_gate = back_mixed * attended * gates * (1.0 - gates)
    score_spec, output_spec, key_spec = score_specs(column)

    def one_crop(pieces):
        q, k, v, shift_row, total_row, back_o = pieces
        scores = (
            jnp.einsum(score_spec, q, k, preferred_element_type=jnp.float32) * score_scale
            + shift_row
        )
        probability = jnp.exp(scores - total_row)
        back_p = jnp.einsum(score_spec, back_o, v, preferred_element_type=jnp.float32)
        centre = jnp.sum(probability * back_p, axis=-1, keepdims=True)
        back_s = (probability * (back_p - centre)).astype(jnp.bfloat16)
        back_q = (
            jnp.einsum(output_spec, back_s, k, preferred_element_type=jnp.float32) * score_scale
        )
        back_k = jnp.einsum(key_spec, back_s, q, preferred_element_type=jnp.float32) * score_scale
        back_v = jnp.einsum(
            key_spec, probability.astype(jnp.bfloat16), back_o, preferred_element_type=jnp.float32
        )
        return (back_q, back_k, back_v)

    back_q, back_k, back_v = lax.map(
        one_crop, (queries, keys_all, values, key_shift, log_total, back_attended)
    )
    back_h = jnp.concatenate(
        [merge_heads(back_q), merge_heads(back_k), merge_heads(back_v), back_gate], axis=-1
    ).astype(jnp.bfloat16)
    back_gate_shift = jnp.sum(back_gate, axis=(0, 1, 2))
    back_in_w = jnp.einsum("bxyc,bxyf->cf", a, back_h, preferred_element_type=jnp.float32)
    back_a = jnp.einsum("bxyf,cf->bxyc", back_h, weight_in, preferred_element_type=jnp.float32)
    return (back_a, back_in_w, back_gate_shift, back_out_w)


def layer_forward(x, key_shift, pair_mask, weights):
    (
        gains,
        offsets,
        attend_mats,
        gate_shift,
        output_mats,
        output_shift,
        expand_mat,
        expand_shift,
        contract_mat,
        contract_shift,
    ) = weights
    normed_row = layer_norm(x, gains[0], offsets[0]).astype(jnp.bfloat16)
    branch_row, saved_row = attend_forward(
        normed_row, attend_mats[0], gate_shift[0], output_mats[0], key_shift, False
    )
    x_one = x + (branch_row + output_shift[0]) * pair_mask
    normed_mid = layer_norm(x_one, gains[1], offsets[1]).astype(jnp.bfloat16)
    normed_col = lax.all_to_all(normed_mid, "seq", split_axis=2, concat_axis=1, tiled=True)
    branch_col, saved_col = attend_forward(
        normed_col, attend_mats[1], gate_shift[1], output_mats[1], key_shift, True
    )
    branch_back = lax.all_to_all(
        branch_col.astype(jnp.bfloat16), "seq", split_axis=1, concat_axis=2, tiled=True
    )
    x_two = x_one + (branch_back.astype(jnp.float32) + output_shift[1]) * pair_mask
    normed_feed = layer_norm(x_two, gains[2], offsets[2]).astype(jnp.bfloat16)
    t = (
        jnp.einsum("bxyc,cf->bxyf", normed_feed, expand_mat, preferred_element_type=jnp.float32)
        + expand_shift
    )
    r = smooth_gate(t).astype(jnp.bfloat16)
    branch_feed = jnp.einsum("bxyf,fc->bxyc", r, contract_mat, preferred_element_type=jnp.float32)
    x_three = x_two + (branch_feed + contract_shift) * pair_mask
    return (x_three, (x_one, x_two, normed_row, saved_row, normed_col, saved_col))


def layer_backward(x, back_x, key_shift, pair_mask, weights, kept_items):
    (
        gains,
        offsets,
        attend_mats,
        gate_shift,
        output_mats,
        output_shift,
        expand_mat,
        expand_shift,
        contract_mat,
        contract_shift,
    ) = weights
    x_one, x_two, normed_row, saved_row, normed_col, saved_col = kept_items
    normed_feed, norm_pull = jax.vjp(layer_norm, x_two, gains[2], offsets[2])
    normed_feed = normed_feed.astype(jnp.bfloat16)
    t = (
        jnp.einsum("bxyc,cf->bxyf", normed_feed, expand_mat, preferred_element_type=jnp.float32)
        + expand_shift
    )
    activated, gate_pull = jax.vjp(smooth_gate, t)
    r = activated.astype(jnp.bfloat16)
    back_y = back_x * pair_mask
    back_contract_shift = jnp.sum(back_y, axis=(0, 1, 2))
    back_branch = back_y.astype(jnp.bfloat16)
    back_contract = jnp.einsum("bxyf,bxyc->fc", r, back_branch, preferred_element_type=jnp.float32)
    back_r = jnp.einsum(
        "bxyc,fc->bxyf", back_branch, contract_mat, preferred_element_type=jnp.float32
    )
    back_t = gate_pull(back_r)[0].astype(jnp.bfloat16)
    back_expand_shift = jnp.sum(back_t.astype(jnp.float32), axis=(0, 1, 2))
    back_expand = jnp.einsum(
        "bxyc,bxyf->cf", normed_feed, back_t, preferred_element_type=jnp.float32
    )
    back_normed = jnp.einsum(
        "bxyf,cf->bxyc", back_t, expand_mat, preferred_element_type=jnp.float32
    )
    back_state, gain_two, offset_two = norm_pull(back_normed)
    back_two = back_x + back_state
    back_y = back_two * pair_mask
    output_shift_one = jnp.sum(back_y, axis=(0, 1, 2))
    back_col = lax.all_to_all(
        back_y.astype(jnp.bfloat16), "seq", split_axis=2, concat_axis=1, tiled=True
    )
    back_a_col, in_one, gate_one, out_one = attend_backward(
        normed_col, attend_mats[1], output_mats[1], key_shift, saved_col, back_col, True
    )
    back_mid = lax.all_to_all(
        back_a_col.astype(jnp.bfloat16), "seq", split_axis=1, concat_axis=2, tiled=True
    ).astype(jnp.float32)
    _, norm_pull = jax.vjp(layer_norm, x_one, gains[1], offsets[1])
    back_state, gain_one, offset_one = norm_pull(back_mid)
    back_one = back_two + back_state
    back_y = back_one * pair_mask
    output_shift_zero = jnp.sum(back_y, axis=(0, 1, 2))
    back_a_row, in_zero, gate_zero, out_zero = attend_backward(
        normed_row,
        attend_mats[0],
        output_mats[0],
        key_shift,
        saved_row,
        back_y.astype(jnp.bfloat16),
        False,
    )
    _, norm_pull = jax.vjp(layer_norm, x, gains[0], offsets[0])
    back_state, gain_zero, offset_zero = norm_pull(back_a_row)
    back_input = back_one + back_state
    gradients = (
        jnp.stack([gain_zero, gain_one, gain_two]),
        jnp.stack([offset_zero, offset_one, offset_two]),
        jnp.stack([in_zero, in_one]),
        jnp.stack([gate_zero, gate_one]),
        jnp.stack([out_zero, out_one]),
        jnp.stack([output_shift_zero, output_shift_one]),
        back_expand,
        back_expand_shift,
        back_contract,
        back_contract_shift,
    )
    return (back_input, gradients)


def body(
    pair_state,
    crop_lengths,
    norm_gain,
    norm_shift,
    attend_weight,
    gate_bias,
    attend_output,
    output_bias,
    expand_weight,
    expand_bias,
    contract_weight,
    contract_bias,
    cotangent,
):
    lengths = crop_lengths[0]
    local_rows = pair_state.shape[1]
    row_ids = lax.axis_index("seq") * local_rows + jnp.arange(local_rows, dtype=jnp.int32)
    col_ids = jnp.arange(pair_state.shape[2], dtype=jnp.int32)
    row_inside = row_ids[None, :] < lengths[:, None]
    col_inside = col_ids[None, :] < lengths[:, None]
    pair_mask = (row_inside[:, :, None] & col_inside[:, None, :]).astype(jnp.float32)[..., None]
    key_shift = jnp.where(col_inside, 0.0, neg_big).astype(jnp.float32)[:, None, None, None, :]
    weights_all = (
        norm_gain,
        norm_shift,
        attend_weight,
        gate_bias,
        attend_output,
        output_bias,
        expand_weight,
        expand_bias,
        contract_weight,
        contract_bias,
    )

    def weights_at(depth_index):
        return tuple((w[depth_index] for w in weights_all))

    x = pair_state.astype(jnp.float32)
    inputs = []
    stored = []
    for depth_index in range(LAYERS):
        inputs.append(x)
        x, kept_items = layer_forward(x, key_shift, pair_mask, weights_at(depth_index))
        stored.append(kept_items)
    pair_output = x.astype(jnp.bfloat16)
    back_x = cotangent.astype(jnp.float32)
    per_layer = [None] * LAYERS
    for depth_index in reversed(range(LAYERS)):
        _, kept_items = layer_forward(
            inputs[depth_index], key_shift, pair_mask, weights_at(depth_index)
        )
        back_x, gradients = layer_backward(
            inputs[depth_index], back_x, key_shift, pair_mask, weights_at(depth_index), kept_items
        )
        per_layer[depth_index] = gradients
    stacked = tuple(
        (jnp.stack([per_layer[depth][number] for depth in range(LAYERS)]) for number in range(10))
    )
    stacked = lax.psum(
        (
            stacked[0],
            stacked[1],
            stacked[2],
            stacked[3],
            stacked[4],
            stacked[5],
            stacked[6],
            stacked[7],
            stacked[8],
            stacked[9],
        ),
        ("seq", "crop"),
    )
    return (
        pair_output,
        back_x,
        stacked[0],
        stacked[1],
        stacked[2],
        stacked[3],
        stacked[4],
        stacked[5],
        stacked[6],
        stacked[7],
        stacked[8],
        stacked[9],
    )


def solution(mesh):
    placed = (
        P("crop", "seq", None, None),
        P("crop", None),
        P(),
        P(),
        P(),
        P(),
        P(),
        P(),
        P(),
        P(),
        P(),
        P(),
        P("crop", "seq", None, None),
    )
    return jax.shard_map(
        body,
        mesh=mesh,
        in_specs=placed,
        out_specs=(
            P("crop", "seq", None, None),
            P("crop", "seq", None, None),
            P(),
            P(),
            P(),
            P(),
            P(),
            P(),
            P(),
            P(),
            P(),
            P(),
        ),
        check_vma=False,
    )
```

profile of v0, /device:TPU:0, one launch (start us, length us, event | category | flops | bytes accessed | tf_op | source)
XLA Modules:
  0.0 3790.7 jit_solution(5747189974514809550)
XLA Ops:
  24.5 23.4 fusion.598
  80.8 96.3 %while.152 = (s32[]{:T(128)}, f32[2,32,256,4,32]{2,4,3,1,0:T(8,128)}, f32[2,32,4,256,1]{3,2,1,4,0:T(4,128)S(1)}, bf16[2,32,256,4,32]{2,4,3,1,0:T(8,128)(2,1)}, b...) while((s32[]{:T(128)}, ...), condition=%wide.region_55.56_spmd, body=%wide.region_52.55_spmd.sunk | while | flops 1174372352 | bytes 112204904 | solution.py:62
  204.7 70.9 %while.144 = (s32[]{:T(128)}, f32[2,32,256,4,32]{2,4,3,1,0:T(8,128)}, bf16[2,32,256,4,32]{2,4,3,1,0:T(8,128)(2,1)}, bf16[2,32,256,4,32]{2,4,3,1,0:T(8,128)(2,1)}...) while((s32[]{:T(128)}, f32[2,32,256,4,32]{2,4,3,1,0:T(8,128)}, ...), condition=%wide.region_5.6_spmd, body=%wide.region_2.5_spmd.sunk | while | flops 1124073728 | bytes 77861976 | solution.py:62
  328.7 85.3 %all-to-all-done.8 = bf16[2,32,256,128]{3,1,0,2:T(8,128)(2,1)} async-done(((bf16[2,32,256,128]{3,1,0,2:T(8,128)(2,1)}), bf16[2,32,256,128]{3,1,0,2:T(8,128)(2,1)}, u32[]{:S(2)}, u32[]{:S(2)}) %all-to-all-start.8) | async-done | bytes 4194336 | tf_op jit(solution)/shard_map/all_to_all | solution.py:132
  424.1 22.8 fusion.601
  479.7 96.5 %while.153 = (s32[]{:T(128)}, f32[2,256,32,4,32]{1,4,3,2,0:T(8,128)}, f32[2,32,4,256,1]{3,2,1,4,0:T(4,128)S(1)}, bf16[2,256,32,4,32]{1,4,3,2,0:T(8,128)(2,1)}, b...) while((s32[]{:T(128)}, ...), condition=%wide.region_61.62_spmd, body=%wide.region_58.61_spmd.sunk | while | flops 1174372352 | bytes 112204904 | solution.py:62
  612.9 22.8 fusion.602
  668.4 71.1 %while.145 = (s32[]{:T(128)}, f32[2,256,32,4,32]{1,4,3,2,0:T(8,128)}, bf16[2,256,32,4,32]{1,4,3,2,0:T(8,128)(2,1)}, bf16[2,256,32,4,32]{1,4,3,2,0:T(8,128)(2,1)}...) while((s32[]{:T(128)}, f32[2,256,32,4,32]{1,4,3,2,0:T(8,128)}, ...), condition=%wide.region_11.12_spmd, body=%wide.region_8.11_spmd.sunk | while | flops 1124073728 | bytes 77861976 | solution.py:62
  786.5 72.8 %all-to-all-done.1 = bf16[2,256,32,128]{3,2,0,1:T(8,128)(2,1)} async-done(((bf16[2,256,32,128]{3,2,0,1:T(8,128)(2,1)}), bf16[2,256,32,128]{3,2,0,1:T(8,128)(2,1)}, u32[]{:S(2)}, u32[]{:S(2)}) %all-to-all-start.1) | async-done | bytes 4194336 | tf_op jit(solution)/shard_map/all_to_all | solution.py:136
  901.1 22.1 fusion.603
  981.7 96.3 %while.148 = (s32[]{:T(128)}, f32[2,32,256,4,32]{2,4,3,1,0:T(8,128)}, f32[2,32,4,256,1]{3,2,1,4,0:T(4,128)S(1)}, bf16[2,32,256,4,32]{2,4,3,1,0:T(8,128)(2,1)}, b...) while((s32[]{:T(128)}, ...), condition=%wide.region_31.32_spmd, body=%wide.region_28.31_spmd.sunk | while | flops 1174372352 | bytes 112204904 | solution.py:62
  1105.3 71.2 %while.146 = (s32[]{:T(128)}, f32[2,32,256,4,32]{2,4,3,1,0:T(8,128)}, bf16[2,32,256,4,32]{2,4,3,1,0:T(8,128)(2,1)}, bf16[2,32,256,4,32]{2,4,3,1,0:T(8,128)(2,1)}...) while((s32[]{:T(128)}, f32[2,32,256,4,32]{2,4,3,1,0:T(8,128)}, ...), condition=%wide.region_19.20_spmd, body=%wide.region_16.19_spmd.sunk | while | flops 1124073728 | bytes 77861976 | solution.py:62
  1227.8 84.6 %all-to-all-done.4 = bf16[2,32,256,128]{3,1,0,2:T(8,128)(2,1)} async-done(((bf16[2,32,256,128]{3,1,0,2:T(8,128)(2,1)}), bf16[2,32,256,128]{3,1,0,2:T(8,128)(2,1)}, u32[]{:S(2)}, u32[]{:S(2)}) %all-to-all-start.4) | async-done | bytes 4194336 | tf_op jit(solution)/shard_map/all_to_all | solution.py:132
  1322.5 22.8 fusion.609
  1377.9 96.2 %while.149 = (s32[]{:T(128)}, f32[2,256,32,4,32]{1,4,3,2,0:T(8,128)}, f32[2,32,4,256,1]{3,2,1,4,0:T(4,128)S(1)}, bf16[2,256,32,4,32]{1,4,3,2,0:T(8,128)(2,1)}, b...) while((s32[]{:T(128)}, ...), condition=%wide.region_37.38_spmd, body=%wide.region_34.37_spmd.sunk | while | flops 1174372352 | bytes 112204904 | solution.py:62
  1510.8 22.8 fusion.610
  1566.1 70.7 %while.147 = (s32[]{:T(128)}, f32[2,256,32,4,32]{1,4,3,2,0:T(8,128)}, bf16[2,256,32,4,32]{1,4,3,2,0:T(8,128)(2,1)}, bf16[2,256,32,4,32]{1,4,3,2,0:T(8,128)(2,1)}...) while((s32[]{:T(128)}, f32[2,256,32,4,32]{1,4,3,2,0:T(8,128)}, ...), condition=%wide.region_25.26_spmd, body=%wide.region_22.25_spmd.sunk | while | flops 1124073728 | bytes 77861976 | solution.py:62
  1688.7 67.7 %all-to-all-done.3 = bf16[2,256,32,128]{3,2,0,1:T(8,128)(2,1)} async-done(((bf16[2,256,32,128]{3,2,0,1:T(8,128)(2,1)}), bf16[2,256,32,128]{3,2,0,1:T(8,128)(2,1)}, u32[]{:S(2)}, u32[]{:S(2)}) %all-to-all-start.3) | async-done | bytes 4194336 | tf_op jit(solution)/shard_map/all_to_all | solution.py:136
  1815.4 35.9 convert_reduce_fusion
  1909.8 85.5 %all-to-all-done.6 = bf16[2,32,256,128]{3,1,0,2:T(8,128)(2,1)} async-done(((bf16[2,32,256,128]{3,1,0,2:T(8,128)(2,1)}), bf16[2,32,256,128]{3,1,0,2:T(8,128)(2,1)}, u32[]{:S(2)}, u32[]{:S(2)}) %all-to-all-start.6) | async-done | bytes 4194336 | tf_op jit(solution)/shard_map/all_to_all | solution.py:192
  2017.1 219.4 %while.150 = (s32[]{:T(128)}, bf16[2,256,32,4,32]{1,4,3,2,0:T(8,128)(2,1)}, bf16[2,256,32,4,32]{1,4,3,2,0:T(8,128)(2,1)}, bf16[2,256,32,4,32]{1,4,3,2,0:T(8,128)...) while((s32[]{:T(128)}, ...), condition=%wide.region_44.45_spmd, body=%wide.region_42.44_spmd.sunk | while | flops 2812248064 | bytes 296626336 | solution.py:101
  2035.5 24.4 multiply_reduce_fusion.32
  2059.9 27.7 multiply_convert_fusion.49
  2145.0 24.4 multiply_reduce_fusion.32
  2169.4 27.7 multiply_convert_fusion.49
  2320.2 21.4 fusion.415
  2341.6 24.2 all-to-all-done.7
  2429.4 220.7 %while.151 = (s32[]{:T(128)}, bf16[2,32,256,4,32]{2,4,3,1,0:T(8,128)(2,1)}, bf16[2,32,256,4,32]{2,4,3,1,0:T(8,128)(2,1)}, bf16[2,32,256,4,32]{2,4,3,1,0:T(8,128)...) while((s32[]{:T(128)}, ...), condition=%wide.region_49.50_spmd, body=%wide.region_47.49_spmd.sunk | while | flops 2812248064 | bytes 296626336 | solution.py:101
  2448.2 24.3 multiply_reduce_fusion.33
  2472.5 27.8 multiply_convert_fusion.50
  2558.3 24.3 multiply_reduce_fusion.33
  2582.6 27.8 multiply_convert_fusion.50
  2718.6 36.2 convert_reduce_fusion.1
  2812.5 20.9 add_convert_fusion.4
  2875.5 29.5 all-to-all-done.10
  2926.9 218.8 %while.154 = (s32[]{:T(128)}, bf16[2,256,32,4,32]{1,4,3,2,0:T(8,128)(2,1)}, bf16[2,256,32,4,32]{1,4,3,2,0:T(8,128)(2,1)}, bf16[2,256,32,4,32]{1,4,3,2,0:T(8,128)...) while((s32[]{:T(128)}, ...), condition=%wide.region_68.69_spmd, body=%wide.region_66.68_spmd.sunk | while | flops 2812248064 | bytes 296626336 | solution.py:101
  2945.1 24.2 multiply_reduce_fusion.34
  2969.2 27.7 multiply_convert_fusion.51
  3054.3 24.2 multiply_reduce_fusion.34
  3078.5 27.7 multiply_convert_fusion.51
  3233.2 42.1 %all-to-all-done.11 = bf16[2,256,32,128]{3,2,0,1:T(8,128)(2,1)} async-done(((bf16[2,256,32,128]{3,2,0,1:T(8,128)(2,1)}), bf16[2,256,32,128]{3,2,0,1:T(8,128)(2,1)}, u32[]{:S(2)}, u32[]{:S(2)}) %all-to-all-start.11) | async-done | bytes 4194336 | tf_op jit(solution)/shard_map/all_to_all | solution.py:198
  3349.8 219.1 %while.155 = (s32[]{:T(128)}, bf16[2,32,256,4,32]{2,4,3,1,0:T(8,128)(2,1)}, bf16[2,32,256,4,32]{2,4,3,1,0:T(8,128)(2,1)}, bf16[2,32,256,4,32]{2,4,3,1,0:T(8,128)...) while((s32[]{:T(128)}, ...), condition=%wide.region_73.74_spmd, body=%wide.region_71.73_spmd.sunk | while | flops 2812248064 | bytes 296626336 | solution.py:101
  3368.2 24.2 multiply_reduce_fusion.35
  3392.4 27.7 multiply_convert_fusion.52
  3477.5 24.2 multiply_reduce_fusion.35
  3501.7 27.7 multiply_convert_fusion.52
  3654.2 38.5 %all-reduce = (f32[2,3,128]{2,1,0:T(4,128)S(1)}, f32[2,3,128]{2,1,0:T(4,128)S(1)}, f32[2,2,128]{2,1,0:T(2,128)}, f32[2,2,128]{2,1,0:T(2,128)}, f32[2,512]{1,0:T(2,128)}, /*index=5*/f32[2,128]{1,0:T(2,128)}) all-reduce(f32[2,3,128]{2,1,0:T(4,128)S(1)} %pad_maximum_fusion.28, ...), channel_id=1, replica_groups=mesh['seq'=8,'crop'=4] {'seq','crop'}, use_global_device_ids=true, to_apply=%region_82.83 | all-reduce | flops 3840 | bytes 30720 | tf_op jit(solution)/shard_map/psum | solution.py:293
  3693.9 82.0 %all-reduce.4.cloned.1.call-done = (f32[2,2,128,512]{3,2,1,0:T(8,128)}, f32[2,2,128,128]{3,2,1,0:T(8,128)}, f32[2,128,512]{2,1,0:T(8,128)}, f32[2,512,128]{2,1,0:T(8,128)}) async-done(((f32[2,2,128,512]{3,2,1,0:T(8,128)}, f32[2,2,128,128]{3,2,1,0:T(8,128)}, f32[2,128,512]{2,1,0:T(8,128)}, f32[2,512,128]{2,1,0:T(8,128)}), (f32[2,2,128,512]{3,2,1,0:T(8,128)}, f32[2,2,128,128]{3,2,1,0:T(8,128)}, ...) | async-done | bytes 2359312 | tf_op jit(solution)/shard_map/psum | solution.py:293
  (890 shorter events, 2490.1 us)
Async XLA Ops:
  20.1 27.9 copy-start.77
  23.8 24.1 copy-start.110
  23.9 24.0 copy-start.97
  24.5 23.4 copy-start.148
  24.5 23.4 copy-start.157
  313.5 100.5 %all-to-all-start.8 = ((bf16[2,32,256,128]{3,1,0,2:T(8,128)(2,1)}), bf16[2,32,256,128]{3,1,0,2:T(8,128)(2,1)}, u32[]{:S(2)}, u32[]{:S(2)}) async-start(bf16[2,32,256,128]{3,1,0,2:T(8,128)(2,1)} %copy.560), calls=%async_computation.8 | async-start | bytes 8388608 | tf_op jit(solution)/shard_map/all_to_all | solution.py:132
  414.0 187.4 %all-to-all-start = ((bf16[2,32,256,128]{3,1,0,2:T(8,128)(2,1)}), bf16[2,32,256,128]{3,1,0,2:T(8,128)(2,1)}, u32[]{:S(2)}, u32[]{:S(2)}) async-start(bf16[2,32,256,128]{3,1,0,2:T(8,128)(2,1)} %copy.487), calls=%async_computation | async-start | bytes 8388608 | tf_op jit(solution)/shard_map/all_to_all | solution.py:132
  601.4 160.2 %all-to-all-start.9 = ((bf16[2,256,32,128]{3,2,0,1:T(8,128)(2,1)}), bf16[2,256,32,128]{3,2,0,1:T(8,128)(2,1)}, u32[]{:S(2)}, u32[]{:S(2)}) async-start(bf16[2,256,32,128]{3,2,0,1:T(8,128)(2,1)} %copy.567), calls=%async_computation.9 | async-start | bytes 8388608 | tf_op jit(solution)/shard_map/all_to_all | solution.py:136
  761.7 97.7 %all-to-all-start.1 = ((bf16[2,256,32,128]{3,2,0,1:T(8,128)(2,1)}), bf16[2,256,32,128]{3,2,0,1:T(8,128)(2,1)}, u32[]{:S(2)}, u32[]{:S(2)}) async-start(bf16[2,256,32,128]{3,2,0,1:T(8,128)(2,1)} %copy.494), calls=%async_computation.1 | async-start | bytes 8388608 | tf_op jit(solution)/shard_map/all_to_all | solution.py:136
  769.1 132.0 %copy-start.195 = (f32[1,512]{1,0:T(1,128)}, f32[1,512]{1,0:T(1,128)S(1)}, u32[]{:S(2)}) copy-start(f32[1,512]{1,0:T(1,128)S(1)} %get-tuple-element.968) | copy-start | bytes 6148
  923.3 25.8 copy-start.85
  928.3 20.7 copy-start.114
  928.4 20.7 copy-start.107
  1215.3 97.1 %all-to-all-start.4 = ((bf16[2,32,256,128]{3,1,0,2:T(8,128)(2,1)}), bf16[2,32,256,128]{3,1,0,2:T(8,128)(2,1)}, u32[]{:S(2)}, u32[]{:S(2)}) async-start(bf16[2,32,256,128]{3,1,0,2:T(8,128)(2,1)} %copy.521), calls=%async_computation.4 | async-start | bytes 8388608 | tf_op jit(solution)/shard_map/all_to_all | solution.py:132
  1312.4 187.0 %all-to-all-start.2 = ((bf16[2,32,256,128]{3,1,0,2:T(8,128)(2,1)}), bf16[2,32,256,128]{3,1,0,2:T(8,128)(2,1)}, u32[]{:S(2)}, u32[]{:S(2)}) async-start(bf16[2,32,256,128]{3,1,0,2:T(8,128)(2,1)} %copy.506), calls=%async_computation.2 | async-start | bytes 8388608 | tf_op jit(solution)/shard_map/all_to_all | solution.py:132
  1499.5 159.2 %all-to-all-start.5 = ((bf16[2,256,32,128]{3,2,0,1:T(8,128)(2,1)}), bf16[2,256,32,128]{3,2,0,1:T(8,128)(2,1)}, u32[]{:S(2)}, u32[]{:S(2)}) async-start(bf16[2,256,32,128]{3,2,0,1:T(8,128)(2,1)} %copy.528), calls=%async_computation.5 | async-start | bytes 8388608 | tf_op jit(solution)/shard_map/all_to_all | solution.py:136
  1658.7 97.7 %all-to-all-start.3 = ((bf16[2,256,32,128]{3,2,0,1:T(8,128)(2,1)}), bf16[2,256,32,128]{3,2,0,1:T(8,128)(2,1)}, u32[]{:S(2)}, u32[]{:S(2)}) async-start(bf16[2,256,32,128]{3,2,0,1:T(8,128)(2,1)} %copy.513), calls=%async_computation.3 | async-start | bytes 8388608 | tf_op jit(solution)/shard_map/all_to_all | solution.py:136
  1792.7 84.3 %copy-start.62 = (f32[2,32,256]{2,1,0:T(8,128)}, f32[2,32,256]{2,1,0:T(8,128)S(1)}, u32[]{:S(2)}) copy-start(f32[2,32,256]{2,1,0:T(8,128)S(1)} %broadcast_multiply_fusion.2) | copy-start | bytes 196612
  1797.8 17.6 copy-start.119
  1797.8 79.2 %copy-start.75 = (f32[2,32,256]{2,1,0:T(8,128)}, f32[2,32,256]{2,1,0:T(8,128)S(1)}, u32[]{:S(2)}) copy-start(f32[2,32,256]{2,1,0:T(8,128)S(1)} %fusion.477) | copy-start | bytes 196612
  1797.9 17.5 copy-start.198
  1797.9 17.5 copy-start.219
  1898.2 97.1 %all-to-all-start.6 = ((bf16[2,32,256,128]{3,1,0,2:T(8,128)(2,1)}), bf16[2,32,256,128]{3,1,0,2:T(8,128)(2,1)}, u32[]{:S(2)}, u32[]{:S(2)}) async-start(bf16[2,32,256,128]{3,1,0,2:T(8,128)(2,1)} %copy.535), calls=%async_computation.6 | async-start | bytes 8388608 | tf_op jit(solution)/shard_map/all_to_all | solution.py:192
  1907.9 90.8 %copy-start.182 = (f32[128]{0:T(128)S(1)}, f32[128]{0:T(128)}, u32[]{:S(2)}) copy-start(f32[128]{0:T(128)} %get-tuple-element.1038) | copy-start | bytes 1540
  2017.5 18.0 copy-start.13
  2127.0 18.0 copy-start.13
  2268.7 97.1 %all-to-all-start.7 = ((bf16[2,256,32,128]{3,2,0,1:T(8,128)(2,1)}), bf16[2,256,32,128]{3,2,0,1:T(8,128)(2,1)}, u32[]{:S(2)}, u32[]{:S(2)}) async-start(bf16[2,256,32,128]{3,2,0,1:T(8,128)(2,1)} %copy.545), calls=%async_computation.7 | async-start | bytes 8388608 | tf_op jit(solution)/shard_map/all_to_all | solution.py:198
  2291.8 22.0 copy-start.48
  2296.7 17.2 copy-start.125
  2429.5 18.7 copy-start.14
  2539.6 18.7 copy-start.14
  2690.7 19.3 slice-start.8
  2690.7 19.3 slice-start.12
  2718.6 36.2 copy-start.96
  2772.1 18.3 slice-start.2
  2807.9 97.1 %all-to-all-start.10 = ((bf16[2,32,256,128]{3,1,0,2:T(8,128)(2,1)}), bf16[2,32,256,128]{3,1,0,2:T(8,128)(2,1)}, u32[]{:S(2)}, u32[]{:S(2)}) async-start(bf16[2,32,256,128]{3,1,0,2:T(8,128)(2,1)} %copy.575), calls=%async_computation.10 | async-start | bytes 8388608 | tf_op jit(solution)/shard_map/all_to_all | solution.py:192
  2875.5 32.9 copy-start.176
  2927.0 18.0 copy-start.15
  3036.3 18.0 copy-start.15
  3178.3 97.1 %all-to-all-start.11 = ((bf16[2,256,32,128]{3,2,0,1:T(8,128)(2,1)}), bf16[2,256,32,128]{3,2,0,1:T(8,128)(2,1)}, u32[]{:S(2)}, u32[]{:S(2)}) async-start(bf16[2,256,32,128]{3,2,0,1:T(8,128)(2,1)} %copy.585), calls=%async_computation.11 | async-start | bytes 8388608 | tf_op jit(solution)/shard_map/all_to_all | solution.py:198
  3182.8 593.1 %all-reduce.4.cloned.1.call-start = ((), (), s32[]{:S(2)}) async-start(), calls=%async_computation.12 | async-start | bytes 4718592 | tf_op jit(solution)/shard_map/psum | solution.py:293
  3198.5 20.9 copy-start.129
  3292.3 19.3 slice-start.4
  3292.3 19.3 slice-start.16
  3311.6 17.9 copy-start.173
  3350.2 18.0 copy-start.12
  3459.5 18.0 copy-start.12
  3588.1 18.8 slice-start.18
  (210 other events, 1818.6 us)
Sparse Core Ops, SparseCore 0:
  3640.7 135.1 all-reduce.3
where the time goes:
time: 3810 us; the launch traced here: 3790 us
  matrix products  1740 us (46%)
  local copies, waits for them, and re-layouts  695 us (18%)
  other arithmetic  656 us (17%)
  waiting for transfers between devices  574 us (15%)
  starting transfers between devices  63.6 us (2%)
  blocking collectives  38.5 us (1%)
    dot_general x16, matrix products, one_crop(): jnp.einsum(score_spec, q, k, preferred_element_type=jnp.float32)  274 us
    dot_general x16, matrix products, one_crop(): jnp.einsum(output_spec, probability, v, preferred_element_type=jnp.float32)  267 us
    convert_element_type x8, other arithmetic, one_crop(): back_s = (probability * (back_p - centre)).astype(jnp.bfloat16)  222 us
    dot_general x8, matrix products, one_crop(): jnp.einsum(score_spec, back_o, v, preferred_element_type=jnp.float32)  194 us
    all_to_all x4, waiting for transfers between devices, layer_forward(): lax.all_to_all(normed_mid, 'seq', split_axis=2, concat_axis=1, tiled=True)  170 us
    sub x8, matrix products, one_crop(): powers = jnp.exp(scores - highest)  153 us
    reshape x20, local copies, waits for them, and re-layouts, merge_heads(): return t.reshape(t.shape[:-2] + (t.shape[-2] * t.shape[-1],))  148 us
    all_to_all x4, waiting for transfers between devices, layer_forward(): lax.all_to_all(branch_col.astype(jnp.bfloat16), 'seq', split_axis=1, conc...  141 us
  transfers between devices with their start and end apart: 13, of which 9 were waited for; matrix products, arithmetic and copies ran while one was open for 24% of the time, Pallas kernels for 0%

commit v1 on v0

v1 whole, which is shorter than its diff:
```python
import functools

import jax
import jax.numpy as jnp
from jax import lax
from jax.experimental import pallas as pl
from jax.experimental.pallas import tpu as pltpu
from jax.sharding import PartitionSpec as P

HEADS = 4
LOG2E = 1.4426950408889634
LN2 = 0.6931471805599453
GELU_A = 0.7978845608028654
GELU_B = 0.7978845608028654 * 0.044715
VMEM_BYTES = 63 * 1024 * 1024
CHUNK = 64
FORMS = {
    "cols_forward": (4, 1, 1),
    "away_forward": (8, 8, 0),
    "cols_middle": (8, 2, 4),
    "away_backward": (4, 4, 0),
    "cols_backward": (8, 2, 3),
    "rows_backward": (8, 1, 1),
}

f32 = jnp.float32
bf16 = jnp.bfloat16


def dot_nn(a, b):
    return lax.dot_general(a, b, (((1,), (0,)), ((), ())), preferred_element_type=f32)


def dot_nt(a, b):
    return lax.dot_general(a, b, (((1,), (1,)), ((), ())), preferred_element_type=f32)


def normalise(x):
    centred = x - jnp.mean(x, axis=0, keepdims=True)
    rstd = lax.rsqrt(jnp.mean(centred * centred, axis=0, keepdims=True) + 1e-5)
    return centred * rstd, rstd


def normalise_back(dy, unit, rstd, gain):
    scaled = dy * gain
    m1 = jnp.mean(scaled, axis=0, keepdims=True)
    m2 = jnp.mean(scaled * unit, axis=0, keepdims=True)
    return rstd * (scaled - m1 - unit * m2)


def row_live(L, length):
    return lax.broadcasted_iota(jnp.int32, (1, L), 1) < length


def rows_of(t, lead):
    t = t.T
    rows = t.shape[0] // functools.reduce(lambda x, y: x * y, lead)
    return t.reshape(lead + (rows, t.shape[1])).astype(bf16)


def pad_head(t, h, C):
    D = C // HEADS
    parts = []
    if h > 0:
        parts.append(jnp.zeros((h * D, t.shape[1]), bf16))
    parts.append(t[h * D : (h + 1) * D])
    if h < HEADS - 1:
        parts.append(jnp.zeros((C - (h + 1) * D, t.shape[1]), bf16))
    return jnp.concatenate(parts, axis=0)


def project(a, w_t, gate_b, length):
    C, L = a.shape
    h_t = dot_nn(w_t, a)
    yield
    live = row_live(L, length)
    keys = h_t[C : 2 * C]
    q_t = (h_t[:C] * (LOG2E * (C // HEADS) ** -0.5)).astype(bf16)
    k_t = jnp.where(live, keys, 0.0).astype(bf16)
    v_t = jnp.where(live, h_t[2 * C : 3 * C], 0.0)
    k = jnp.where(live, keys, keys[:, 0:1]).T.astype(bf16)
    g_t = 0.5 * jnp.tanh(0.5 * (h_t[3 * C :] + gate_b)) + 0.5
    return k, v_t.T.astype(bf16), q_t, k_t, v_t.astype(bf16), g_t


def chunk_of(opts):
    return 128 if "long" in opts else CHUNK


def in_chunks(rows, chunk, fn):
    if chunk is None:
        return fn(slice(0, rows))
    parts = [fn(slice(i, i + chunk)) for i in range(0, rows, chunk)]
    if isinstance(parts[0], tuple):
        return tuple(jnp.concatenate(p, axis=0) for p in zip(*parts))
    return jnp.concatenate(parts, axis=0)


def attend(k, q_t, v_t, length, chunk, lean):
    L, C = k.shape
    D = C // HEADS
    ones = jnp.where(row_live(L, length), 1.0, 0.0)
    ones = jnp.broadcast_to(ones, (16, L)).astype(bf16)
    scores = [dot_nn(k, pad_head(q_t, h, C)) for h in range(HEADS)]
    yield
    outs, powers, sums, mixes, tops = [], [], [], [], []
    for h in range(HEADS):
        s_t = scores[h]
        top = jnp.max(s_t, axis=0, keepdims=True)
        p = in_chunks(L, chunk, lambda r: jnp.exp2(s_t[r] - top).astype(bf16))
        powers.append(p)
        tops.append(top)
        mixes.append(dot_nn(jnp.concatenate([v_t[h * D : (h + 1) * D], ones], axis=0), p))
        if h % 2 == 1:
            yield
    for h in range(HEADS):
        o = mixes[h]
        inv = 1.0 / o[D : D + 1]
        outs.append(o[:D] * inv)
        sums.append(inv)
        if lean:
            tops[h] = tops[h] + jnp.log2(o[D : D + 1])
    return jnp.concatenate(outs, axis=0), powers, sums, tops


def attend_back(dz, a, kept, w, wo, length, chunk, dz_n, a_n):
    v, q_t, k_t, g_t, mixed_t, powers, sums = kept
    C, L = q_t.shape
    D = C // HEADS
    dmixed = dot_nn(wo, dz) if dz is not None else dot_nt(wo, dz_n)
    d_wo = dot_nt(mixed_t, dz) if dz_n is None else dot_nn(mixed_t, dz_n)
    lean = not isinstance(powers, list)
    if lean:
        scores = [dot_nn(powers, pad_head(q_t, h, C)) for h in range(HEADS)]
    yield
    g = g_t.astype(f32)
    both = dmixed * mixed_t.astype(f32)
    dgate = both * (1.0 - g)
    do = dmixed * g
    live_row = row_live(L, length)
    dps, centres, dos = [], [], []
    for h in range(HEADS):
        rows = slice(h * D, (h + 1) * D)
        scale = 1.0 if lean else sums[h]
        do_h = (do[rows] * scale).astype(bf16)
        centres.append(jnp.sum(both[rows], axis=0, keepdims=True) * scale)
        parts = []
        if h > 0:
            parts.append(jnp.zeros((h * D, L), bf16))
        parts.append(do_h)
        if h < HEADS - 1:
            parts.append(jnp.zeros((C - (h + 1) * D, L), bf16))
        dps.append(dot_nn(v, jnp.concatenate(parts, axis=0)))
        dos.append(do_h)
    yield
    dq, dk, dv = [], [], []
    for h in range(HEADS):
        rows = slice(h * D, (h + 1) * D)
        dp, centre = dps[h], centres[h]
        if lean:
            s_t, log = scores[h], sums[h]
            p = in_chunks(L, chunk, lambda r: jnp.exp2(s_t[r] - log).astype(bf16))
        else:
            p = powers[h][...]
        ds = in_chunks(L, chunk, lambda r: p[r] * (dp[r] - centre).astype(bf16))
        dv.append(dot_nt(dos[h], p))
        dk.append(dot_nt(q_t[rows], ds))
        dq.append(dot_nn(k_t[rows], ds))
        if h % 2 == 1:
            yield
    dq = jnp.concatenate(dq, axis=0) * (D**-0.5)
    dk = jnp.where(live_row, jnp.concatenate(dk, axis=0) * LN2, 0.0)
    dv = jnp.where(live_row, jnp.concatenate(dv, axis=0), 0.0)
    dh = jnp.concatenate([dq, dk, dv, dgate], axis=0).astype(bf16)
    da = dot_nn(w, dh)
    d_w = dot_nt(dh, a) if a_n is None else dot_nn(dh, a_n)
    yield
    return da, d_w, d_wo, dgate


def lane_fold(t):
    out = t[:, :128]
    for j in range(1, t.shape[1] // 128):
        out = out + t[:, j * 128 : (j + 1) * 128]
    return out


VECTORS = ("gain0", "shift0", "gain1", "shift1", "gain2", "shift2", "bo0", "bo1", "gate0", "gate1", "bc")


class Weights:
    def __init__(self, refs, m, feed, L):
        self.columns, self.next_columns = refs[0].at[0], refs[1].at[0]
        self.w, self.w_t, self.wo, self.wo_t = (r.at[0, 0] for r in refs[2:6])
        if feed:
            self.we, self.wc, self.we_t, self.wc_t = (r.at[0] for r in refs[6:10])
        self.m, self.L, self.made = m, L, {}

    def column(self, ref, key, i):
        if key not in self.made:
            t = ref[...][:, i : i + 1]
            self.made[key] = jnp.broadcast_to(t, (t.shape[0], self.L))
        return self.made[key]

    def vector(self, name):
        return self.column(self.columns, name, VECTORS.index(name))

    def norm(self, n):
        return self.vector(f"gain{n}"), self.vector(f"shift{n}")

    def norm_of_next(self):
        return self.column(self.next_columns, "next0", 0), self.column(self.next_columns, "next1", 1)

    def expand_bias(self, rows):
        C = self.columns.shape[0]
        block, start = divmod(rows.start, C)
        t = self.column(self.columns, block, len(VECTORS) + block)
        return t[start : start + rows.stop - rows.start]


def weight_inputs(arrays, l, m, feed):
    vectors = arrays[0]

    def layer(a):
        return (a, (1,) + a.shape[1:], lambda *_: (l,) + (0,) * (a.ndim - 1))

    def branch(a):
        return (a, (1, 1) + a.shape[2:], lambda *_: (l, m) + (0,) * (a.ndim - 2))

    out = [layer(vectors), (vectors, (1,) + vectors.shape[1:], lambda *_: (1, 0, 0))]
    out += [branch(a) for a in arrays[1:5]]
    if feed:
        out += [layer(a) for a in arrays[5:9]]
    return out


def unpack(block, scratch, width, offset):
    peers, count, S, C = block.shape

    def step(p, _):
        part = block[p].astype(f32).reshape(count * S, C)
        at = pl.multiple_of((p * width + offset) * S, 8)
        scratch[pl.ds(at, count * S), :] = part
        return 0

    lax.fori_loop(0, peers, step, 0)


def pick(scratch, s, L, S):
    return scratch[pl.ds(s, L, stride=S), :]


SAVED = ("v", "q_t", "k_t", "g_t", "mix_t", "p", "sums")
LEAN = ("v", "q_t", "k_t", "g_t", "mix_t", "k", "sums")


def load_saved(refs, at, lean=False):
    v, q_t, k_t, g_t, mixed_t = [r[at] for r in refs[:5]]
    sums = [refs[6][at + (slice(h, h + 1), slice(None))] for h in range(HEADS)]
    if lean:
        return v, q_t, k_t, g_t, mixed_t, refs[5][at], sums
    powers = [refs[5].at[at + (h,)] for h in range(HEADS)]
    return v, q_t, k_t, g_t, mixed_t, powers, sums


def attention_forward(a, wts, length, saved=None, at=None, lean=False):
    gate_b = wts.vector(f"gate{wts.m}")
    k, v, q_t, k_t, v_t, g_t = yield from project(a, wts.w_t[...], gate_b, length)
    g_b = g_t.astype(bf16)
    if saved is not None:
        for ref, value in zip(saved, (v, q_t, k_t, g_b)):
            ref[at] = value
    o_t, powers, sums, logs = yield from attend(k, q_t, v_t, length, CHUNK, lean)
    mixed_t = (o_t * g_t).astype(bf16)
    z = dot_nn(wts.wo_t[...], mixed_t)
    if saved is not None:
        saved[4][at] = mixed_t
        if lean:
            saved[5][at] = k
        for h in range(HEADS):
            if not lean:
                saved[5][at + (h,)] = powers[h]
            saved[6][at + (slice(h, h + 1), slice(None))] = logs[h] if lean else sums[h]
    yield
    return z, (v, q_t, k_t, g_b, mixed_t, powers, sums)


def attention_backward(dz, a, wts, length, kept, acc, dz_n=None, a_n=None, opts=()):
    da, d_w, d_wo, dgate = yield from attend_back(
        dz, a, kept, wts.w[...], wts.wo[...], length, chunk_of(opts), dz_n, a_n
    )
    acc.add("d_w", d_w)
    acc.add("d_wo", d_wo)
    acc.add("d_gate", lane_fold(dgate))
    return da


def turned(opts, dz, a, wts, length, kept, acc):
    if "turn" in opts:
        return attention_backward(dz, a, wts, length, kept, acc, dz.T, a.T, opts)
    return attention_backward(dz, a, wts, length, kept, acc, opts=opts)


def gelu_half(t, bias):
    u = (t + bias).astype(bf16)
    u2 = u * u
    return u * bf16(0.5), u2, jnp.tanh(u * (bf16(GELU_A) + bf16(GELU_B) * u2))


def activate(t, wts):
    def part(r):
        u_half, _, th = gelu_half(t[r], wts.expand_bias(r))
        return u_half * th + u_half

    return in_chunks(t.shape[0], CHUNK, part)


def activate_back(t, dr, wts):
    def part(r):
        u_half, u2, th = gelu_half(t[r], wts.expand_bias(r))
        r_part = u_half * th + u_half
        left = bf16(0.5) - bf16(0.5) * th
        slope = (bf16(1.0) - left) + r_part * left * (bf16(2.0 * GELU_A) + bf16(6.0 * GELU_B) * u2)
        return r_part, dr[r].astype(bf16) * slope

    return in_chunks(t.shape[0], CHUNK, part)


def with_ones(t):
    return jnp.concatenate([t, jnp.ones((16, t.shape[1]), t.dtype)], axis=0)


def feed_gradients(acc, dz, r, a2, dt, opts):
    d_wc = dot_nn(r, dz.T) if "turn" in opts else dot_nt(r, dz)
    d_we = dot_nt(with_ones(a2), dt)
    yield
    C = a2.shape[0]
    acc.add("d_wc", d_wc)
    acc.add("d_we", d_we[:C])
    acc.add("d_be", d_we[C : C + 8])


BLOCKS = ("d_w", "d_wo", "d_wc", "d_we")


def acc_layout(names, C, F):
    shapes = {"d_w": (4 * C, C), "d_wo": (C, C), "d_be": (8, F), "d_wc": (F, C), "d_we": (C, F)}
    layout, at = {}, 0
    for name in names:
        rows, cols = shapes.get(name, (C, 128))
        layout[name] = (at, rows, cols // 128)
        at += rows * (cols // 128)
    return layout, at


def packed_layout(names, C, F):
    layout, _ = acc_layout(names, C, F)
    out, at = {}, 0
    for name in names:
        if name in BLOCKS:
            out[name] = at
            at += layout[name][1] * layout[name][2]
    row = at
    for name in names:
        if name not in BLOCKS:
            out[name] = row
            row += F // 128 if name == "d_be" else 1
    return out, at + 16


def pack(sums, names, rows, C, F):
    def body(*refs):
        out, at = refs[-1], 0
        for ref, kernel in zip(refs, names):
            layout, _ = acc_layout(kernel, C, F)
            vectors = []
            for name in kernel:
                first, count, blocks = layout[name]
                if name in BLOCKS:
                    for i in range(0, count * blocks, 128):
                        out[at : at + 128, :] = ref[first + i : first + i + 128, :].astype(bf16)
                        at += 128
                elif name == "d_be":
                    vectors += [ref[first + j * 8 : first + j * 8 + 1, :] for j in range(blocks)]
                else:
                    t = ref[first : first + count, :]
                    vectors.append(jnp.sum(t.T, axis=0, keepdims=True))
            vectors += [jnp.zeros((16 - len(vectors), 128), f32)]
            out[at : at + 16, :] = jnp.concatenate(vectors, axis=0).astype(bf16)
            at += 16
        if at < rows:
            out[at:, :] = jnp.zeros((rows - at, 128), bf16)

    return pl.pallas_call(
        body,
        out_shape=jax.ShapeDtypeStruct((rows, 128), bf16),
        compiler_params=pltpu.CompilerParams(vmem_limit_bytes=VMEM_BYTES),
        name="pack",
    )(*sums)


class Acc:
    def __init__(self, ref, layout):
        self.ref, self.layout = ref, layout

    def add(self, name, value):
        at, rows, blocks = self.layout[name]
        for j in range(blocks):
            self.ref[at + j * rows : at + (j + 1) * rows, :] += value[:, j * 128 : (j + 1) * 128]


def run(kernel, name, grid, info, inputs, weights, outputs, scratch, flops, names=(), before=None, into=(), wait=()):
    arrays, l, m, feed = weights
    C, F = arrays[5].shape[-2:]
    into = dict(into)
    ins_w = weight_inputs(arrays, l, m, feed)
    L = arrays[9]
    layout, rows = acc_layout(names, C, F)
    const = lambda *_: (0, 0)
    ins_b = [(before, (rows, 128), const)] if before is not None else []
    all_ins = list(inputs) + ins_w + ins_b
    outs = list(outputs) + ([((rows, 128), f32, (rows, 128), const)] if names else [])
    n_in, n_w = len(inputs), len(ins_w)

    def body(info_ref, *refs):
        ins = refs[:n_in]
        wts = Weights(refs[n_in : n_in + n_w], m, feed, L)
        rest = refs[len(all_ins) + len(into) + len(wait) :]
        acc = None
        if names:
            total = rest[len(outputs)]
            acc = Acc(total, layout)
            first = pl.program_id(0) == 0
            for d in range(1, len(grid)):
                first = first & (pl.program_id(d) == 0)

            @pl.when(first)
            def _():
                if before is not None:
                    total[...] = refs[n_in + n_w][...]
                else:
                    total[...] = jnp.zeros_like(total)

        kernel(info_ref, ins, wts, rest[: len(outputs)], acc, rest[len(outs) :])

    moved = sum(a.size * a.dtype.itemsize for a, _, _ in all_ins)
    moved += sum(4 * s[0] * s[1] if len(s) == 2 else 2 * functools.reduce(lambda x, y: x * y, s) for s, _, _, _ in outs)
    res = pl.pallas_call(
        body,
        grid_spec=pltpu.PrefetchScalarGridSpec(
            num_scalar_prefetch=1,
            grid=grid,
            in_specs=[pl.BlockSpec(b, i) for _, b, i in all_ins]
            + [pl.BlockSpec(memory_space=pl.ANY)] * (len(into) + len(wait)),
            out_specs=[pl.BlockSpec(b, i) for _, _, b, i in outs],
            scratch_shapes=scratch,
        ),
        out_shape=[jax.ShapeDtypeStruct(s, d) for s, d, _, _ in outs],
        compiler_params=pltpu.CompilerParams(
            vmem_limit_bytes=VMEM_BYTES,
            dimension_semantics=("arbitrary",) * len(grid),
        ),
        cost_estimate=pl.CostEstimate(flops=int(flops), bytes_accessed=int(moved), transcendentals=0),
        input_output_aliases={1 + len(all_ins) + i: o for i, o in enumerate(into)},
        name=name,
    )(info, *[a for a, _, _ in all_ins], *[into[o] for o in into], *wait)
    return res


def clip(form, most):
    return (min(form[0], most),) + form[1:]


def saved_outputs(lead, lead_block, index, L, C, names=SAVED):
    out = []
    for name in names:
        tail, dt = ((L, C), bf16) if name in ("v", "k") else ((C, L), bf16)
        if name == "p":
            tail = (HEADS, L, L)
        if name == "sums":
            tail, dt = (HEADS, L), f32
        more = lambda *g, extra=len(tail) - 2: index(*g) + (0,) * extra
        out.append((lead + tail, dt, lead_block + tail, more))
    return out


def together(form, body):
    count, width, lag = form[:3]
    waiting = [(s // width * lag, body(s)) for s in range(count)]
    turn = 0
    while waiting:
        waiting = [(t, g) for t, g in waiting if t > turn or next(g, g) is not g]
        turn += 1


HOME = (
    "d_w", "d_wo", "d_gate", "d_bo", "d_gain", "d_shift", "d_gain2", "d_shift2",
    "d_bc", "d_be", "d_wc", "d_we",
)
NAMES_MIDDLE = HOME + ("d_bo0",)
NAMES_COLS = HOME + ("d_gain0", "d_shift0")
NAMES_AWAY = ("d_w", "d_wo", "d_gate")
NAMES_ROWS = NAMES_AWAY + ("d_bo", "d_gain", "d_shift")


def body(
    pair_state,
    crop_lengths,
    norm_gain,
    norm_shift,
    attend_weight,
    gate_bias,
    attend_output,
    output_bias,
    expand_weight,
    expand_bias,
    contract_weight,
    contract_bias,
    cotangent,
):
    B, R, L, C = pair_state.shape
    F = expand_weight.shape[-1]
    n, crops = lax.axis_size("seq"), lax.axis_size("crop")
    half = n // B
    M = 2 * half
    W = L // M
    parts = 2 if W % 32 == 0 else 1
    K = W // parts
    RP = 2 if R % 32 == 0 else 1
    S, SR = min(16, K), min(16, R // RP)
    both = ("seq", "crop")
    pairs = range(0, crops, 2)
    wide = [[s * crops + p + c for s in range(n) for c in range(2)] for p in pairs]
    near = [
        [s * crops + p + c for s in range(b * half, (b + 1) * half) for c in range(2)]
        for p in pairs
        for b in range(B)
    ]

    vectors = [norm_gain[:, 0], norm_shift[:, 0], norm_gain[:, 1], norm_shift[:, 1]]
    vectors += [norm_gain[:, 2], norm_shift[:, 2], output_bias[:, 0], output_bias[:, 1]]
    vectors += [gate_bias[:, 0], gate_bias[:, 1], contract_bias]
    vectors = jnp.concatenate([jnp.stack(vectors, axis=1), expand_bias.reshape(-1, F // C, C)], axis=1)
    arrays = (
        jnp.swapaxes(jnp.pad(vectors, ((0, 0), (0, 128 - vectors.shape[1]), (0, 0))), 1, 2),
        attend_weight,
        jnp.swapaxes(attend_weight, 2, 3),
        attend_output,
        jnp.swapaxes(attend_output, 2, 3),
        expand_weight,
        contract_weight,
        jnp.swapaxes(expand_weight, 1, 2),
        jnp.swapaxes(contract_weight, 1, 2),
        L,
    )
    me, group = lax.axis_index("seq"), lax.axis_index("crop")
    lens = crop_lengths[0].astype(jnp.int32)
    other = lax.ppermute(lens, "crop", [(c, c ^ 1) for c in range(crops)])
    info_rows = jnp.concatenate([lens, (me * R).astype(jnp.int32)[None]])
    first_col = ((me % half) * 2 + group % 2) * W
    info_cols = [
        jnp.stack([jnp.where(group % 2 == t, lens, other)[me // half], first_col.astype(jnp.int32)])
        for t in range(2)
    ]

    def swap(groups, x):
        return lax.all_to_all(
            x, both, split_axis=0, concat_axis=0, tiled=True, axis_index_groups=groups
        )

    def over_wide(x):
        return swap(wide, x.reshape((2 * n,) + x.shape[-3:]))

    def over_near(x):
        return swap(near, x)

    def after(x, y):
        cut = (0,) * x.ndim
        size = (1,) * (x.ndim - 2) + (min(8, x.shape[-2], y.shape[-2]), 128)
        from_y = lax.slice(y, (0,) * y.ndim, (1,) * (y.ndim - 2) + size[-2:])
        mine = lax.slice(x, cut, size) + 0.0 * from_y.reshape(size)
        return lax.dynamic_update_slice(x, mine.astype(x.dtype), cut)

    flops = 60 * 2 * 256**3

    def cot_part(x, c):
        return jnp.swapaxes(x.reshape(B, R, M, parts, K, C)[:, :, :, c], 1, 2)

    last = over_wide(cot_part(cotangent, 0))
    cot = [last]

    form = clip((8, 8, 0), SR)
    G = form[0]

    def rows_forward(info, ins, wts, outs, acc, scr):
        (x_ref,) = ins
        b, step = pl.program_id(0), pl.program_id(1)
        length = info[b]

        def one(s):
            row = info[B] + step * G + s
            x = x_ref[0, s].astype(f32).T
            gain, shift = wts.norm(0)
            unit, _ = normalise(x)
            a = (unit * gain + shift).astype(bf16)
            z, _ = yield from attention_forward(a, wts, length, outs[parts:], (0, s))
            live = row_live(L, jnp.where(row < length, length, 0))
            x1 = x + jnp.where(live, z + wts.vector("bo0"), 0.0)
            x1 = rows_of(x1, (M, parts))
            for c in range(parts):
                outs[c][0, :, s] = x1[:, c]

        together(form, one)

    lead = (B, R)
    at_row = lambda b, i, *_: (b, i, 0, 0)
    x1_spec = ((B, M, R, K, C), bf16, (1, M, G, K, C), lambda b, i, *_: (b, 0, i, 0, 0))
    res = run(
        rows_forward,
        "rows_forward",
        (B, R // G),
        info_rows,
        [(pair_state, (1, G, L, C), at_row)],
        (arrays, 0, 0, False),
        [x1_spec] * parts + saved_outputs(lead, (1, G), at_row, L, C),
        [],
        B * R * flops,
    )
    saved_r0 = res[parts:]
    x1 = [over_wide(after(t, last) if c == 0 else t) for c, t in enumerate(res[:parts])]

    scr_in = pltpu.VMEM((L * S + S, C), f32)

    class Step:
        def __init__(self, form, count, first):
            self.form = clip(form[:3], S)
            self.opts = form[3:]
            G = self.G = self.form[0]
            per = self.per = S // G
            self.first, self.count = first, count
            self.grid = (count // S, per)
            at_col = lambda i, j, *_: (i * per + j, 0, 0)
            at_send = lambda i, j, *_: (0, first // G + i * per + j, 0, 0)
            self.saved = saved_outputs((count,), (G,), at_col, L, C)
            self.lean = saved_outputs((count,), (G,), at_col, L, C, LEAN)
            self.bf16 = ((count, C, L), bf16, (G, C, L), at_col)
            self.rows = ((count, L, C), bf16, (G, L, C), at_col)
            self.send = ((M, W, W, C), bf16, (M, G, W, C), at_send)

        def send_wide(self, t, rows):
            per = self.per
            at = lambda i, j, *_: (0, t, i * per + j, 0, 0)
            return ((n, 2, K, rows, C), bf16, (n, 1, self.G, rows, C), at)

        def wide(self, x, t):
            x = x.reshape((n, 2) + x.shape[1:])
            return (x, (n, 1, R, S, C), lambda i, j, *_: (0, t, 0, i, 0))

        def near(self, x):
            first = self.first // S
            return (x, (M, W, S, C), lambda i, j, *_: (0, 0, first + i, 0))

        def live_at(self, info, s):
            length = info[0]
            step = pl.program_id(0) * self.per + pl.program_id(1)
            column = info[1] + self.first + step * self.G + s
            return length, row_live(L, jnp.where(column < length, length, 0))

        def picked(self, scratch, s):
            return pick(scratch, pl.program_id(1) * self.G + s, L, S)

    def at_first(fill):
        pl.when(pl.program_id(1) == 0)(fill)

    def with_blocks(arrays, specs):
        return [(a, s[2], s[3]) for a, s in zip(arrays, specs)]

    def cols_forward(st, info, ins, wts, outs, acc, scr):
        (x1_ref,) = ins
        a0_out, x1_out, x2_out, x3_out = outs[:4]
        at_first(lambda: unpack(x1_ref.at[:, 0], scr[0], R, 0))

        def one(s):
            length, live = st.live_at(info, s)
            x1 = st.picked(scr[0], s).T
            x1_out[s] = x1.astype(bf16)
            gain, shift = wts.norm(1)
            unit, _ = normalise(x1)
            a = (unit * gain + shift).astype(bf16)
            z, _ = yield from attention_forward(a, wts, length, outs[4:], (s,), True)
            x2 = x1 + jnp.where(live, z + wts.vector("bo1"), 0.0)
            x2_out[s] = x2.astype(bf16)
            gain, shift = wts.norm(2)
            unit, _ = normalise(x2)
            a2 = (unit * gain + shift).astype(bf16)
            t = dot_nn(wts.we_t[...], a2)
            yield
            y = dot_nn(wts.wc_t[...], activate(t, wts))
            yield
            x3 = x2 + jnp.where(live, y + wts.vector("bc"), 0.0)
            x3_out[s] = x3.astype(bf16)
            gain, shift = wts.norm_of_next()
            unit, _ = normalise(x3)
            a0_out[:, s] = rows_of(unit * gain + shift, (M,))

        together(st.form, one)

    a0_send, kept_c0, before_c = [None, None], {}, [cot[0]]
    for c in range(parts):
        for t in range(2):
            st = Step(FORMS["cols_forward"], K, c * K)
            a0_send[t], *kept_c0[t, c] = run(
                functools.partial(cols_forward, st),
                "cols_forward",
                st.grid,
                info_cols[t],
                [st.wide(x1[c], t)],
                (arrays, 0, 1, True),
                [st.send, st.bf16, st.bf16, st.bf16] + st.lean,
                [scr_in],
                K * flops * 2,
                into={0: a0_send[t]} if c else {},
                wait=before_c,
            )
            before_c = [kept_c0[t, c][0]]
    a0 = []
    for t in range(2):
        a0.append(over_near(a0_send[t]))

    def away_forward(st, info, ins, wts, outs, acc, scr):
        z_out, a0_out = outs[:2]
        at_first(lambda: unpack(ins[0], scr[0], W, 0))

        def one(s):
            a = st.picked(scr[0], s)
            a0_out[s] = a.astype(bf16)
            a = a.T.astype(bf16)
            z, _ = yield from attention_forward(a, wts, info[0], outs[2:], (s,))
            z_out[:, s] = rows_of(z, (M,))

        together(st.form, one)

    z0, kept_r1 = [], []
    for t in range(2):
        st = Step(FORMS["away_forward"], W, 0)
        z_send, *kept = run(
            functools.partial(away_forward, st),
            "away_forward",
            st.grid,
            info_cols[t],
            [st.near(a0[t])],
            (arrays, 1, 0, False),
            [st.send, st.rows] + st.saved,
            [scr_in],
            W * flops,
            wait=[k[0] for k in kept_r1],
        )
        z0.append(over_near(z_send))
        kept_r1.append(kept)

    def cols_middle(st, info, ins, wts, outs, acc, scr):
        z_ref, cot_ref, x_ref = ins
        dz_send, out_send, dx_out = outs

        def fill():
            unpack(z_ref, scr[0], W, 0)
            unpack(cot_ref.at[:, 0], scr[1], R, 0)

        at_first(fill)

        def one(s):
            length, live = st.live_at(info, s)
            z0 = st.picked(scr[0], s).T
            x1 = x_ref[s].astype(f32) + jnp.where(live, z0 + wts.vector("bo0"), 0.0)
            gain1, shift1 = wts.norm(1)
            unit1, rstd1 = normalise(x1)
            a1 = (unit1 * gain1 + shift1).astype(bf16)
            z, kept = yield from attention_forward(a1, wts, length)
            x2 = x1 + jnp.where(live, z + wts.vector("bo1"), 0.0)
            gain2, shift2 = wts.norm(2)
            unit2, rstd2 = normalise(x2)
            a2 = (unit2 * gain2 + shift2).astype(bf16)
            t = dot_nn(wts.we_t[...], a2)
            dx = st.picked(scr[1], s).T
            dy = jnp.where(live, dx, 0.0)
            dz = dy.astype(bf16)
            dr = dot_nn(wts.wc[...], dz)
            acc.add("d_bc", lane_fold(dy))
            yield
            r, dt = activate_back(t, dr, wts)
            y = dot_nn(wts.wc_t[...], r)
            da2 = dot_nn(wts.we[...], dt)
            yield from feed_gradients(acc, dz, r, a2, dt, st.opts)
            x3 = x2 + jnp.where(live, y + wts.vector("bc"), 0.0)
            out_send[:, 0, s] = rows_of(x3, (n,))
            acc.add("d_gain2", lane_fold(da2 * unit2))
            acc.add("d_shift2", lane_fold(da2))
            dx = dx + normalise_back(da2, unit2, rstd2, gain2)
            dy = jnp.where(live, dx, 0.0)
            acc.add("d_bo", lane_fold(dy))
            da1 = yield from turned(st.opts, dy.astype(bf16), a1, wts, length, kept, acc)
            acc.add("d_gain", lane_fold(da1 * unit1))
            acc.add("d_shift", lane_fold(da1))
            dx = dx + normalise_back(da1, unit1, rstd1, gain1)
            dx_out[s] = dx.astype(bf16)
            dy = jnp.where(live, dx, 0.0)
            acc.add("d_bo0", lane_fold(dy))
            dz_send[:, s] = rows_of(dy, (M,))

        together(st.form, one)

    if parts > 1:
        later, _ = lax.optimization_barrier((cotangent, x1[0]))
        cot.append(over_wide(cot_part(later, 1)))
    dz_send, out_sends, dx1, sum_m = [None, None], [], {}, None
    dz0, out_rows = [], []
    for c in range(parts):
        out_send = None
        for t in range(2):
            st = Step(FORMS["cols_middle"], K, c * K)
            into = {0: dz_send[t]} if c else {}
            if t:
                into[1] = out_send
            dz_send[t], out_send, dx1[t, c], sum_m = run(
                functools.partial(cols_middle, st),
                "cols_middle",
                st.grid,
                info_cols[t],
                [st.near(z0[t]), st.wide(cot[c], t), (kept_c0[t, c][2], (st.G, C, L), st.bf16[3])],
                (arrays, 1, 1, True),
                [st.send, st.send_wide(t, R), st.bf16],
                [scr_in, scr_in],
                K * flops * 4,
                NAMES_MIDDLE,
                sum_m,
                into,
                out_rows if t else [],
            )
        out_sends.append(out_send)
        if c == 0:
            out_rows.append(over_wide(out_send))
    for t in range(2):
        dz0.append(over_near(dz_send[t]))

    def away_backward(st, info, ins, wts, outs, acc, scr):
        (da_send,) = outs
        a_ref = ins[1]
        at_first(lambda: unpack(ins[0], scr[0], W, 0))

        def one(s):
            dz_n = st.picked(scr[0], s)
            dz = dz_n.T.astype(bf16) if "turn" in st.opts else None
            dz_n = dz_n.astype(bf16)
            kept = load_saved(ins[2:], (s,))
            da = yield from attention_backward(
                dz, None, wts, info[0], kept, acc, dz_n, a_ref[s], st.opts
            )
            da_send[:, s] = rows_of(da, (M,))

        together(st.form, one)

    da0, sum_r1 = [], None
    for t in range(2):
        st = Step(FORMS["away_backward"], W, 0)
        da_send, sum_r1 = run(
            functools.partial(away_backward, st),
            "away_backward",
            st.grid,
            info_cols[t],
            [st.near(dz0[t])] + with_blocks(kept_r1[t], [st.rows] + st.saved),
            (arrays, 1, 0, False),
            [st.send],
            [scr_in],
            W * flops * 2,
            NAMES_AWAY,
            sum_r1,
        )
        last = over_near(da_send)
        da0.append(last)

    def cols_backward(st, info, ins, wts, outs, acc, scr):
        da_ref, dx_ref, x1_ref, x2_ref, x3_ref = ins[:5]
        at_first(lambda: unpack(da_ref, scr[0], W, 0))

        def one(s):
            length, live = st.live_at(info, s)
            da0 = st.picked(scr[0], s).T
            gain, _ = wts.norm_of_next()
            unit, rstd = normalise(x3_ref[s].astype(f32))
            acc.add("d_gain0", lane_fold(da0 * unit))
            acc.add("d_shift0", lane_fold(da0))
            dx = dx_ref[s].astype(f32) + normalise_back(da0, unit, rstd, gain)
            dy = jnp.where(live, dx, 0.0)
            gain2, shift2 = wts.norm(2)
            unit2, rstd2 = normalise(x2_ref[s].astype(f32))
            a2 = (unit2 * gain2 + shift2).astype(bf16)
            t = dot_nn(wts.we_t[...], a2)
            dz = dy.astype(bf16)
            dr = dot_nn(wts.wc[...], dz)
            acc.add("d_bc", lane_fold(dy))
            yield
            r, dt = activate_back(t, dr, wts)
            da2 = dot_nn(wts.we[...], dt)
            yield from feed_gradients(acc, dz, r, a2, dt, st.opts)
            acc.add("d_gain2", lane_fold(da2 * unit2))
            acc.add("d_shift2", lane_fold(da2))
            dx = dx + normalise_back(da2, unit2, rstd2, gain2)
            dy = jnp.where(live, dx, 0.0)
            acc.add("d_bo", lane_fold(dy))
            gain1, shift1 = wts.norm(1)
            unit1, rstd1 = normalise(x1_ref[s].astype(f32))
            a1 = (unit1 * gain1 + shift1).astype(bf16)
            kept = load_saved(ins[5:], (s,), True)
            da1 = yield from turned(st.opts, dy.astype(bf16), a1, wts, length, kept, acc)
            acc.add("d_gain", lane_fold(da1 * unit1))
            acc.add("d_shift", lane_fold(da1))
            dx = dx + normalise_back(da1, unit1, rstd1, gain1)
            dx = rows_of(dx, (n, len(outs)))
            for part, dx_send in enumerate(outs):
                dx_send[:, 0, s] = dx[:, part]

        together(st.form, one)

    if parts > 1:
        last = over_wide(after(out_sends[1], last))
        out_rows.append(last)
    dx_rows, sum_c0 = [], None
    for c in range(parts):
        pieces = RP if c == parts - 1 else 1
        dx_sends = []
        for t in range(2):
            st = Step(FORMS["cols_backward"], K, c * K)
            *dx_sends, sum_c0 = run(
                functools.partial(cols_backward, st),
                "cols_backward",
                st.grid,
                info_cols[t],
                [st.near(da0[t]), (dx1[t, c], (st.G, C, L), st.bf16[3])]
                + with_blocks(kept_c0[t, c], [st.bf16, st.bf16, st.bf16] + st.lean),
                (arrays, 0, 1, True),
                [st.send_wide(t, R // pieces)] * pieces,
                [scr_in],
                K * flops * 3,
                NAMES_COLS,
                sum_c0,
                dict(enumerate(dx_sends)),
            )
        sent = []
        for x in dx_sends:
            last = over_wide(after(x, last))
            sent.append(last.reshape((B, M) + last.shape[1:]))
        dx_rows.append(sent)

    def rows_backward(part, form, info, ins, wts, outs, acc, scr):
        x_ref = ins[parts]
        grad_out = outs[0]
        G = form[0]
        per = SR // G
        i, j = pl.program_id(1), pl.program_id(2)
        length = info[pl.program_id(0)]

        def fill():
            for c in range(parts):
                unpack(ins[c].at[0], scr[0], W, c * K)

        pl.when(j == 0)(fill)

        def one(s):
            row = info[B] + part * (R // RP) + (i * per + j) * G + s
            live = row_live(L, jnp.where(row < length, length, 0))
            dx = pick(scr[0], j * G + s, L, SR).T
            dy = jnp.where(live, dx, 0.0)
            acc.add("d_bo", lane_fold(dy))
            gain, shift = wts.norm(0)
            unit, rstd = normalise(x_ref[0, s].astype(f32).T)
            a = (unit * gain + shift).astype(bf16)
            kept = load_saved(ins[parts + 1 : parts + 1 + len(SAVED)], (0, s))
            da = yield from turned(form[3:], dy.astype(bf16), a, wts, length, kept, acc)
            acc.add("d_gain", lane_fold(da * unit))
            acc.add("d_shift", lane_fold(da))
            grad_out[0, s] = (dx + normalise_back(da, unit, rstd, gain)).T

        together(form, one)

    packed = [sum_m, sum_r1, sum_c0]
    pair_grad, sum_r0 = None, None
    for part in range(RP):
        form = clip(FORMS["rows_backward"], SR)
        G = form[0]
        per, steps = SR // G, R // RP // G
        at_row3 = lambda b, i, j, *_, o=part * steps: (b, o + i * per + j, 0, 0)
        sent = []
        for pieces in dx_rows:
            offset = part * (R // RP // SR) if len(pieces) == 1 else 0
            piece = pieces[0] if len(pieces) == 1 else pieces[part]
            sent.append(
                (piece, (1, M, K, SR, C), lambda b, i, j, *_, o=offset: (b, 0, 0, o + i, 0))
            )
        pair_grad, sum_r0 = run(
            functools.partial(rows_backward, part, form),
            "rows_backward",
            (B, R // RP // SR, per),
            info_rows,
            sent
            + [(pair_state, (1, G, L, C), at_row3)]
            + with_blocks(saved_r0, saved_outputs(lead, (1, G), at_row3, L, C)),
            (arrays, 0, 0, False),
            [((B, R, L, C), f32, (1, G, L, C), at_row3)],
            [pltpu.VMEM((L * SR + SR, C), f32)],
            B * (R // RP) * flops * 2,
            NAMES_ROWS,
            sum_r0,
            {0: pair_grad} if part else {},
        )
    out = jnp.stack([x.reshape(B, M, K, R, C) for x in out_rows], axis=2)
    pair_output = jnp.transpose(out.reshape(B, L, R, C), (0, 2, 1, 3))

    devices = n * crops

    def for_all(sums, names):
        rows = sum(packed_layout(x, C, F)[1] for x in names)
        rows = -(-rows // (devices * 16)) * 16
        return pack(sums, names, devices * rows, C, F).reshape(devices, rows, 128)

    def exchange(x):
        got = lax.all_to_all(x, both, 0, 0, tiled=True)
        return jnp.sum(got.astype(f32), axis=0)

    def spread(x, groups):
        x = jnp.broadcast_to(x, (len(groups[0]),) + x.shape)
        return swap(groups, x)

    first = for_all(packed, (NAMES_MIDDLE, NAMES_AWAY, NAMES_COLS))
    large = exchange(after(first, last))
    small = exchange(after(for_all([sum_r0], (NAMES_ROWS,)), large[None]))
    mine = jnp.concatenate([large, small], axis=0).astype(bf16)
    lines = [[s * crops + q for s in range(x, n, 2)] for x in range(2) for q in range(crops)]
    planes = [[s * crops + q for s in (z, z + 1) for q in range(crops)] for z in range(0, n, 2)]
    whole = spread(spread(mine, lines), planes)
    whole = whole.reshape(2 * crops, n // 2, mine.shape[0], 128)
    grads = assemble(whole, large.shape[0], C, F)
    gain, shift = (jnp.swapaxes(t, 0, 1) for t in grads[:2])
    return (pair_output, pair_grad, gain, shift) + tuple(grads[2:])


def assemble(whole, split, C, F):
    per_plane, planes, rows, _ = whole.shape
    tail_rows = rows - split
    names = (NAMES_MIDDLE, NAMES_AWAY, NAMES_COLS, NAMES_ROWS)
    layouts = [packed_layout(x, C, F) for x in names]
    bases = [0, layouts[0][1], layouts[0][1] + layouts[1][1]]

    def body(x_ref, gain, shift, w, gate, wo, bo, we, be, wc, bc, big, tail):
        def step(i, _):
            for z in range(planes):
                part = x_ref[i, z].astype(f32)
                at = z * per_plane + i
                big[pl.ds(pl.multiple_of(at * split, 16), split), :] = part[:split]
                tail[pl.ds(pl.multiple_of(at * tail_rows, 16), tail_rows), :] = part[split:]
            return 0

        lax.fori_loop(0, per_plane, step, 0)

        def get(kernel, name, count=1, offset=0):
            at = layouts[kernel][0][name] + offset
            if kernel == 3:
                return tail[at : at + count, :]
            return big[bases[kernel] + at : bases[kernel] + at + count, :]

        M, A, N, R = range(4)
        for l, m, kernel in ((0, 0, R), (0, 1, N), (1, 0, A), (1, 1, M)):
            for j in range(4):
                w[l, m, :, j * C : (j + 1) * C] = get(kernel, "d_w", C, j * C).T
            wo[l, m] = get(kernel, "d_wo", C)
            gate[l, m : m + 1, :] = get(kernel, "d_gate")
        for l, m, kernel, name in ((0, 0, R, "d_bo"), (0, 1, N, "d_bo"), (1, 0, M, "d_bo0"), (1, 1, M, "d_bo")):
            bo[l, m : m + 1, :] = get(kernel, name)
        where = ((0, 0, R, ""), (0, 1, N, ""), (0, 2, N, "2"), (1, 0, N, "0"), (1, 1, M, ""), (1, 2, M, "2"))
        for l, i, kernel, end in where:
            gain[i, l : l + 1, :] = get(kernel, "d_gain" + end)
            shift[i, l : l + 1, :] = get(kernel, "d_shift" + end)
        for l, kernel in ((0, N), (1, M)):
            bc[l : l + 1, :] = get(kernel, "d_bc")
            wc[l] = get(kernel, "d_wc", F)
            for j in range(F // 128):
                lanes = slice(j * 128, (j + 1) * 128)
                we[l, :, lanes] = get(kernel, "d_we", C, j * C)
                be[l : l + 1, lanes] = get(kernel, "d_be", 1, j)

    shapes = [(3, 2, C), (3, 2, C), (2, 2, C, 4 * C), (2, 2, C), (2, 2, C, C), (2, 2, C)]
    shapes += [(2, C, F), (2, F), (2, F, C), (2, C)]
    return pl.pallas_call(
        body,
        out_shape=[jax.ShapeDtypeStruct(s, f32) for s in shapes],
        scratch_shapes=[
            pltpu.VMEM((per_plane * planes * split, 128), f32),
            pltpu.VMEM((per_plane * planes * tail_rows, 128), f32),
        ],
        compiler_params=pltpu.CompilerParams(vmem_limit_bytes=VMEM_BYTES),
        name="assemble",
    )(whole)


def solution(mesh):
    placed = P("crop", "seq", None, None)
    return jax.shard_map(
        body,
        mesh=mesh,
        in_specs=(placed, P("crop", None)) + (P(),) * 10 + (placed,),
        out_specs=(placed, placed) + (P(),) * 10,
        check_vma=False,
    )
```

time: 3810 us -> 842 us (0.22)
  matrix products: 1740 us -> 0 us
  local copies, waits for them, and re-layouts: 695 us -> 21 us
  other arithmetic: 656 us -> 15.3 us
  Pallas kernels: 0 us -> 518 us
  waiting for transfers between devices: 574 us -> 125 us
  starting transfers between devices: 63.6 us -> 145 us
    dot_general x106 -> x0, matrix products: 1590 us -> none  [the longest x16 274 us: one_crop(): jnp.einsum(score_spec, q, k, preferred_element_type=jnp.float32)]
    pallas_call x0 -> x22, Pallas kernels: none -> 518 us  [the longest x19 509 us: run(): pl.pallas_call(body, grid_spec=pltpu.PrefetchScalarGridSpec(num_scalar_pr...]
    all_to_all x12 -> x20, waiting for transfers between devices: 492 us -> 125 us  [the longest x18 114 us: swap(): lax.all_to_all(x, both, split_axis=0, concat_axis=0, tiled=True, axis_ind...]
    reduce_sum x36 -> x2, other arithmetic: 317 us -> 1.43 us  [exchange(): return jnp.sum(got.astype(f32), axis=0)]
    convert_element_type x23 -> x0, other arithmetic: 296 us -> none  [the longest x8 222 us: one_crop(): back_s = (probability * (back_p - centre)).astype(jnp.bfloat16)]
    convert_element_type x28 -> x0, local copies, waits for them, and re-layouts: 181 us -> none  [the longest x8 53.1 us: layer_forward(): branch_back.astype(jnp.float32) + output_shift[1]]
    slice x25 -> x9, local copies, waits for them, and re-layouts: 170 us -> 2.79 us  [the longest x1 1.96 us: cot_part(): return jnp.swapaxes(x.reshape(B, R, M, parts, K, C)[:, :, :, c], 1, 2)]
    sub x8 -> x0, matrix products: 153 us -> none  [one_crop(): powers = jnp.exp(scores - highest)]
  transfers between devices with their start and end apart: 13 -> 21, of which waited for: 9 -> 12; matrix products, arithmetic and copies ran while one was open for 24% -> 2% of each run, Pallas kernels for 0% -> 59%
where the time goes in v1:
time: 842 us; the launch traced here: 835 us
  Pallas kernels  518 us (62%)
  starting transfers between devices  145 us (17%)
  waiting for transfers between devices  125 us (15%)
  local copies, waits for them, and re-layouts  21 us (2%)
  other arithmetic  15.3 us (2%)
  blocking collectives  9.42 us (1%)
    pallas_call x19, Pallas kernels, run(): pl.pallas_call(body, grid_spec=pltpu.PrefetchScalarGridSpec(num_scalar_pr...  509 us
    all_to_all x18, starting transfers between devices, swap(): lax.all_to_all(x, both, split_axis=0, concat_axis=0, tiled=True, axis_ind...  133 us
    all_to_all x18, waiting for transfers between devices, swap(): lax.all_to_all(x, both, split_axis=0, concat_axis=0, tiled=True, axis_ind...  114 us
  transfers between devices with their start and end apart: 21, of which 12 were waited for; matrix products, arithmetic and copies ran while one was open for 2% of the time, Pallas kernels for 59%

profile of v1, /device:TPU:0, one launch (start us, length us, event | category | flops | bytes accessed | tf_op | source)
XLA Modules:
  0.0 834.8 jit_solution(9158873978044409363)
XLA Ops:
  4.5 7.6 all-to-all-start.1
  17.0 35.0 %rows_forward.1 = (bf16[2,8,32,16,128]{4,3,2,1,0:T(8,128)(2,1)}, bf16[2,8,32,16,128]{4,3,2,1,0:T(8,128)(2,1)}, bf16[2,32,256,128]{3,2,1,0:T(8,128)(2,1)}, bf16[2...) custom-call(s32[3]{0:T(128)} %pad_add_fusion.1.info_ref, ...), custom_call_target="tpu_custom_call" | custom-call | flops 128849018880 | bytes 64618496 | tf_op jit(solution)/shard_map/rows_forward/pallas_call | solution.py:448
  54.5 11.3 %all-to-all-start.2 = ((bf16[16,32,16,128]{3,2,1,0:T(8,128)(2,1)}), bf16[16,32,16,128]{3,2,1,0:T(8,128)(2,1)S(1)}, u32[]{:S(2)}, u32[]{:S(2)}) async-start(bf16[16,32,16,128]{3,2,1,0:T(8,128)(2,1)} %bitcast.91), calls=%async_computation.2 | async-start | bytes 4194304 | tf_op jit(solution)/shard_map/all_to_all | solution.py:567
  71.0 36.0 %all-to-all-done.2 = bf16[16,32,16,128]{3,2,1,0:T(8,128)(2,1)S(1)} async-done(((bf16[16,32,16,128]{3,2,1,0:T(8,128)(2,1)}), bf16[16,32,16,128]{3,2,1,0:T(8,128)(2,1)S(1)}, u32[]{:S(2)}, u32[]{:S(2)}) %all-to-all-start.2) | async-done | bytes 2097184 | tf_op jit(solution)/shard_map/all_to_all | solution.py:567
  108.3 11.6 %all-to-all-start = ((bf16[16,32,16,128]{3,2,1,0:T(8,128)(2,1)}), bf16[16,32,16,128]{3,2,1,0:T(8,128)(2,1)}, u32[]{:S(2)}, u32[]{:S(2)}) async-start(bf16[16,32,16,128]{3,2,1,0:T(8,128)(2,1)} %bitcast.7), calls=%async_computation | async-start | bytes 4194304 | tf_op jit(solution)/shard_map/all_to_all | solution.py:567
  119.8 20.0 %cols_forward.4 = (bf16[8,32,32,128]{3,2,1,0:T(8,128)(2,1)}, bf16[16,128,256]{2,1,0:T(8,128)(2,1)}, bf16[16,128,256]{2,1,0:T(8,128)(2,1)}, bf16[16,128,256]{2,1,...) custom-call(s32[2]{0:T(128)} %get-tuple-element.253.info_ref, ...), custom_call_target="tpu_custom_call" | custom-call | flops 64424509440 | bytes 16285696 | tf_op jit(solution)/shard_map/cols_forward/pallas_call | solution.py:448
  139.9 20.1 %cols_forward.5 = (bf16[8,32,32,128]{3,2,1,0:T(8,128)(2,1)}, bf16[16,128,256]{2,1,0:T(8,128)(2,1)}, bf16[16,128,256]{2,1,0:T(8,128)(2,1)}, bf16[16,128,256]{2,1,...) custom-call(s32[2]{0:T(128)} %get-tuple-element.252.info_ref, ...), custom_call_target="tpu_custom_call" | custom-call | flops 64424509440 | bytes 16285696 | tf_op jit(solution)/shard_map/cols_forward/pallas_call | solution.py:448
  161.0 20.1 %cols_forward.6 = (bf16[8,32,32,128]{3,2,1,0:T(8,128)(2,1)}, bf16[16,128,256]{2,1,0:T(8,128)(2,1)}, bf16[16,128,256]{2,1,0:T(8,128)(2,1)}, bf16[16,128,256]{2,1,...) custom-call(s32[2]{0:T(128)} %get-tuple-element.253.info_ref, ...), custom_call_target="tpu_custom_call", output_to_operand_aliasing={{0}: (12, {})} | custom-call | flops 64424509440 | bytes 16285696 | tf_op jit(solution)/shard_map/cols_forward/pallas_call | solution.py:448
  181.1 10.9 %all-to-all-start.4 = ((bf16[8,32,32,128]{3,2,1,0:T(8,128)(2,1)}), bf16[8,32,32,128]{3,2,1,0:T(8,128)(2,1)}, u32[]{:S(2)}, u32[]{:S(2)}) async-start(bf16[8,32,32,128]{3,2,1,0:T(8,128)(2,1)} %get-tuple-element.136), calls=%async_computation.4 | async-start | bytes 4194304 | tf_op jit(solution)/shard_map/all_to_all | solution.py:567
  195.8 20.1 %cols_forward.7 = (bf16[8,32,32,128]{3,2,1,0:T(8,128)(2,1)}, bf16[16,128,256]{2,1,0:T(8,128)(2,1)}, bf16[16,128,256]{2,1,0:T(8,128)(2,1)}, bf16[16,128,256]{2,1,...) custom-call(s32[2]{0:T(128)} %get-tuple-element.252.info_ref, ...), custom_call_target="tpu_custom_call", output_to_operand_aliasing={{0}: (12, {})} | custom-call | flops 64424509440 | bytes 16285696 | tf_op jit(solution)/shard_map/cols_forward/pallas_call | solution.py:448
  217.8 4.4 all-to-all-start.3
  222.1 20.2 %away_forward.2 = (bf16[8,32,32,128]{3,2,1,0:T(8,128)(2,1)}, bf16[32,256,128]{2,1,0:T(8,128)(2,1)}, bf16[32,256,128]{2,1,0:T(8,128)(2,1)}, bf16[32,128,256]{2,1,...) custom-call(s32[2]{0:T(128)} %get-tuple-element.253.info_ref, ...), custom_call_target="tpu_custom_call" | custom-call | flops 64424509440 | bytes 35192832 | tf_op jit(solution)/shard_map/away_forward/pallas_call | solution.py:448
  242.4 5.5 all-to-all-done.3.refs_0_
  252.2 20.2 %away_forward.3 = (bf16[8,32,32,128]{3,2,1,0:T(8,128)(2,1)}, bf16[32,256,128]{2,1,0:T(8,128)(2,1)}, bf16[32,256,128]{2,1,0:T(8,128)(2,1)}, bf16[32,128,256]{2,1,...) custom-call(s32[2]{0:T(128)} %get-tuple-element.252.info_ref, ...), custom_call_target="tpu_custom_call" | custom-call | flops 64424509440 | bytes 35192832 | tf_op jit(solution)/shard_map/away_forward/pallas_call | solution.py:448
  272.4 5.5 all-to-all-done.6.refs_0_
  277.9 4.4 all-to-all-start.5
  282.3 31.9 %cols_middle.4 = (bf16[8,32,32,128]{3,2,1,0:T(8,128)(2,1)}, bf16[8,2,16,32,128]{4,3,2,1,0:T(8,128)(2,1)}, bf16[16,128,256]{2,1,0:T(8,128)(2,1)}, f32[2720,128]{1,0:T(8,128)}) custom-call(s32[2]{0:T(128)} %get-tuple-element.253.info_ref, bf16[8,32,32,128]{3,2,1,0:T(8,128)(2,1)} %all-to-all-done.6.refs_0_, bf16[8,2,32,16,128]{4,3,2,1,0:T(8,128)(2,1)} %bitcast.18.refs_1_, ...), custom_call_target="tpu_custom_call" | custom-call | flops 128849018880 | bytes 14499840 | tf_op jit(solution)/shard_map/cols_middle/pallas_call | solution.py:448
  314.1 7.0 all-to-all-start.8
  321.2 32.4 %cols_middle.5 = (bf16[8,32,32,128]{3,2,1,0:T(8,128)(2,1)}, bf16[8,2,16,32,128]{4,3,2,1,0:T(8,128)(2,1)}, bf16[16,128,256]{2,1,0:T(8,128)(2,1)}, f32[2720,128]{1,0:T(8,128)}) custom-call(s32[2]{0:T(128)} %get-tuple-element.252.info_ref, bf16[8,32,32,128]{3,2,1,0:T(8,128)(2,1)} %all-to-all-done.5.refs_0_, ...), custom_call_target="tpu_custom_call", output_to_operand_aliasing={{1}: (15, {})} | custom-call | flops 128849018880 | bytes 15892480 | tf_op jit(solution)/shard_map/cols_middle/pallas_call | solution.py:448
  353.6 8.7 %all-to-all-done.8 = bf16[16,32,16,128]{3,2,1,0:T(8,128)(2,1)} async-done(((bf16[16,32,16,128]{3,2,1,0:T(8,128)(2,1)}), bf16[16,32,16,128]{3,2,1,0:T(8,128)(2,1)}, u32[]{:S(2)}, u32[]{:S(2)}) %all-to-all-start.8) | async-done | bytes 2097184 | tf_op jit(solution)/shard_map/all_to_all | solution.py:567
  362.3 11.3 %all-to-all-start.7 = ((bf16[16,16,32,128]{3,2,1,0:T(8,128)(2,1)}), bf16[16,16,32,128]{3,2,1,0:T(8,128)(2,1)}, u32[]{:S(2)}, u32[]{:S(2)}) async-start(bf16[16,16,32,128]{3,2,1,0:T(8,128)(2,1)} %bitcast.94), calls=%async_computation.7 | async-start | bytes 4194304 | tf_op jit(solution)/shard_map/all_to_all | solution.py:567
  373.6 32.2 %cols_middle.6 = (bf16[8,32,32,128]{3,2,1,0:T(8,128)(2,1)}, bf16[8,2,16,32,128]{4,3,2,1,0:T(8,128)(2,1)}, bf16[16,128,256]{2,1,0:T(8,128)(2,1)}, f32[2720,128]{1,0:T(8,128)}) custom-call(s32[2]{0:T(128)} %get-tuple-element.253.info_ref, bf16[8,32,32,128]{3,2,1,0:T(8,128)(2,1)} %all-to-all-done.6.refs_0_, ...), custom_call_target="tpu_custom_call", output_to_operand_aliasing={{0}: (15, {})} | custom-call | flops 128849018880 | bytes 15892480 | tf_op jit(solution)/shard_map/cols_middle/pallas_call | solution.py:448
  405.9 8.9 %all-to-all-done.7.refs_16_ = bf16[16,16,32,128]{3,2,1,0:T(8,128)(2,1)} async-done(((bf16[16,16,32,128]{3,2,1,0:T(8,128)(2,1)}), bf16[16,16,32,128]{3,2,1,0:T(8,128)(2,1)}, u32[]{:S(2)}, u32[]{:S(2)}) %all-to-all-start.7) | async-done | bytes 2097184 | tf_op jit(solution)/shard_map/all_to_all | solution.py:567
  414.8 10.3 %all-to-all-start.10 = ((bf16[8,32,32,128]{3,2,1,0:T(8,128)(2,1)}), bf16[8,32,32,128]{3,2,1,0:T(8,128)(2,1)}, u32[]{:S(2)}, u32[]{:S(2)}) async-start(bf16[8,32,32,128]{3,2,1,0:T(8,128)(2,1)} %get-tuple-element.163), calls=%async_computation.10 | async-start | bytes 4194304 | tf_op jit(solution)/shard_map/all_to_all | solution.py:567
  425.0 32.6 %cols_middle.7 = (bf16[8,32,32,128]{3,2,1,0:T(8,128)(2,1)}, bf16[8,2,16,32,128]{4,3,2,1,0:T(8,128)(2,1)}, bf16[16,128,256]{2,1,0:T(8,128)(2,1)}, f32[2720,128]{1,0:T(8,128)}) custom-call(s32[2]{0:T(128)} %get-tuple-element.252.info_ref, bf16[8,32,32,128]{3,2,1,0:T(8,128)(2,1)} %all-to-all-done.5.refs_0_, ...), custom_call_target="tpu_custom_call", output_to_operand_aliasing={{0}: (15, {}), {1}: (16, {})} | custom-call | flops 128849018880 | bytes 15892480 | tf_op jit(solution)/shard_map/cols_middle/pallas_call | solution.py:448
  457.7 4.4 all-to-all-start.9
  462.0 29.9 %away_backward.2 = (bf16[8,32,32,128]{3,2,1,0:T(8,128)(2,1)}, f32[768,128]{1,0:T(8,128)}) custom-call(s32[2]{0:T(128)} %get-tuple-element.253.info_ref, bf16[8,32,32,128]{3,2,1,0:T(8,128)(2,1)} %all-to-all-done.10.refs_0_, bf16[32,256,128]{2,1,0:T(8,128)(2,1)} %get-tuple-element.137.refs_7_.refs_1_, bf16[32,256,128]{2,1,0:T(8,128)(2,1)} %get-tuple-element.164.refs_2_, ...), custom_call_target="tpu_custom_call" | custom-call | flops 128849018880 | bytes 35651584 | tf_op jit(solution)/shard_map/away_backward/pallas_call | solution.py:448
  492.0 4.4 all-to-all-start.13
  496.3 30.1 %away_backward.3 = (bf16[8,32,32,128]{3,2,1,0:T(8,128)(2,1)}, f32[768,128]{1,0:T(8,128)}) custom-call(s32[2]{0:T(128)} %get-tuple-element.252.info_ref, bf16[8,32,32,128]{3,2,1,0:T(8,128)(2,1)} %all-to-all-done.9.refs_0_, bf16[32,256,128]{2,1,0:T(8,128)(2,1)} %get-tuple-element.155.refs_1_, bf16[32,256,128]{2,1,0:T(8,128)(2,1)} %get-tuple-element.156.refs_2_, ...), custom_call_target="tpu_custom_call" | custom-call | flops 128849018880 | bytes 36044800 | tf_op jit(solution)/shard_map/away_backward/pallas_call | solution.py:448
  526.5 4.4 all-to-all-start.11
  530.8 25.9 %cols_backward.4 = (bf16[8,2,16,32,128]{4,3,2,1,0:T(8,128)(2,1)}, f32[2848,128]{1,0:T(8,128)}) custom-call(s32[2]{0:T(128)} %get-tuple-element.253.info_ref, bf16[8,32,32,128]{3,2,1,0:T(8,128)(2,1)} %all-to-all-done.13.refs_0_, bf16[16,128,256]{2,1,0:T(8,128)(2,1)} %get-tuple-element.183.refs_1_, bf16[16,128,256]{2,1,0:T(8,128)(2,1)} %get-tuple-element.130.refs_11_.refs_2_, ...), custom_call_target="tpu_custom_call" | custom-call | flops 96636764160 | bytes 18825216 | tf_op jit(solution)/shard_map/cols_backward/pallas_call | solution.py:448
  557.9 7.6 all-to-all-start.12
  565.5 26.5 %cols_backward.5 = (bf16[8,2,16,32,128]{4,3,2,1,0:T(8,128)(2,1)}, f32[2848,128]{1,0:T(8,128)}) custom-call(s32[2]{0:T(128)} %get-tuple-element.252.info_ref, bf16[8,32,32,128]{3,2,1,0:T(8,128)(2,1)} %all-to-all-done.11.refs_0_, bf16[16,128,256]{2,1,0:T(8,128)(2,1)} %get-tuple-element.173.refs_1_, ...), custom_call_target="tpu_custom_call", output_to_operand_aliasing={{0}: (24, {})} | custom-call | flops 96636764160 | bytes 20283392 | tf_op jit(solution)/shard_map/cols_backward/pallas_call | solution.py:448
  592.0 26.7 %cols_backward.6 = (bf16[8,2,16,16,128]{4,3,2,1,0:T(8,128)(2,1)}, bf16[8,2,16,16,128]{4,3,2,1,0:T(8,128)(2,1)}, f32[2848,128]{1,0:T(8,128)}) custom-call(s32[2]{0:T(128)} %get-tuple-element.253.info_ref, bf16[8,32,32,128]{3,2,1,0:T(8,128)(2,1)} %all-to-all-done.13.refs_0_, bf16[16,128,256]{2,1,0:T(8,128)(2,1)} %get-tuple-element.205.refs_1_, ...), custom_call_target="tpu_custom_call" | custom-call | flops 96636764160 | bytes 20283392 | tf_op jit(solution)/shard_map/cols_backward/pallas_call | solution.py:448
  620.0 6.4 all-to-all-start.14
  626.3 26.4 %cols_backward.7 = (bf16[8,2,16,16,128]{4,3,2,1,0:T(8,128)(2,1)}, bf16[8,2,16,16,128]{4,3,2,1,0:T(8,128)(2,1)}, f32[2848,128]{1,0:T(8,128)}) custom-call(s32[2]{0:T(128)} %get-tuple-element.252.info_ref, bf16[8,32,32,128]{3,2,1,0:T(8,128)(2,1)} %all-to-all-done.11.refs_0_, ...), custom_call_target="tpu_custom_call", output_to_operand_aliasing={{0}: (24, {}), {1}: (25, {})} | custom-call | flops 96636764160 | bytes 20283392 | tf_op jit(solution)/shard_map/cols_backward/pallas_call | solution.py:448
  652.8 14.7 %all-to-all-done.14 = bf16[16,16,32,128]{3,2,1,0:T(8,128)(2,1)} async-done(((bf16[16,16,32,128]{3,2,1,0:T(8,128)(2,1)}), bf16[16,16,32,128]{3,2,1,0:T(8,128)(2,1)}, u32[]{:S(2)}, u32[]{:S(2)}) %all-to-all-start.14) | async-done | bytes 2097184 | tf_op jit(solution)/shard_map/all_to_all | solution.py:567
  668.7 11.3 %all-to-all-start.15 = ((bf16[16,16,16,128]{3,2,1,0:T(8,128)(2,1)}), bf16[16,16,16,128]{3,2,1,0:T(8,128)(2,1)}, u32[]{:S(2)}, u32[]{:S(2)}) async-start(bf16[16,16,16,128]{3,2,1,0:T(8,128)(2,1)} %bitcast.96), calls=%async_computation.15 | async-start | bytes 2097152 | tf_op jit(solution)/shard_map/all_to_all | solution.py:567
  683.4 19.7 %all-to-all-done.15 = bf16[16,16,16,128]{3,2,1,0:T(8,128)(2,1)} async-done(((bf16[16,16,16,128]{3,2,1,0:T(8,128)(2,1)}), bf16[16,16,16,128]{3,2,1,0:T(8,128)(2,1)}, u32[]{:S(2)}, u32[]{:S(2)}) %all-to-all-start.15) | async-done | bytes 1048608 | tf_op jit(solution)/shard_map/all_to_all | solution.py:567
  704.3 7.3 all-to-all-start.16
  711.6 29.3 %rows_backward.2 = (f32[2,32,256,128]{3,2,1,0:T(8,128)}, f32[1152,128]{1,0:T(8,128)}) custom-call(s32[3]{0:T(128)} %pad_add_fusion.1.info_ref, bf16[2,8,16,32,128]{4,3,2,1,0:T(8,128)(2,1)} %bitcast.33.refs_0_, bf16[2,8,16,16,128]{4,3,2,1,0:T(8,128)(2,1)} %bitcast.39.refs_1_, bf16[2,32,256,128]{3,2,1,0:T(8,128)(2,1)} %refs_2_.3, ...), custom_call_target="tpu_custom_call" | custom-call | flops 128849018880 | bytes 68485120 | tf_op jit(solution)/shard_map/rows_backward/pallas_call | solution.py:448
  742.3 6.2 all-to-all-start.17
  748.4 29.5 %rows_backward.3 = (f32[2,32,256,128]{3,2,1,0:T(8,128)}, f32[1152,128]{1,0:T(8,128)}) custom-call(s32[3]{0:T(128)} %pad_add_fusion.1.info_ref, bf16[2,8,16,32,128]{4,3,2,1,0:T(8,128)(2,1)} %bitcast.33.refs_0_, bf16[2,8,16,16,128]{4,3,2,1,0:T(8,128)(2,1)} %bitcast.38.refs_1_, bf16[2,32,256,128]{3,2,1,0:T(8,128)(2,1)} %refs_2_.3, ...), custom_call_target="tpu_custom_call", output_to_operand_aliasing={{0}: (18, {})} | custom-call | flops 128849018880 | bytes 69074944 | tf_op jit(solution)/shard_map/rows_backward/pallas_call | solution.py:448
  782.5 5.8 all-to-all-start.18
  788.3 10.6 %all-to-all-done.18 = bf16[32,32,128]{2,1,0:T(8,128)(2,1)S(1)} async-done(((bf16[32,32,128]{2,1,0:T(8,128)(2,1)}), bf16[32,32,128]{2,1,0:T(8,128)(2,1)S(1)}, u32[]{:S(2)}, u32[]{:S(2)}) %all-to-all-start.18) | async-done | bytes 262176 | tf_op jit(solution)/shard_map/all_to_all | solution.py:1026
  798.9 9.4 %all_to_all.105 = bf16[4,160,128]{2,1,0:T(8,128)(2,1)S(1)} all-to-all(bf16[4,160,128]{2,1,0:T(8,128)(2,1)S(1)} %broadcast_in_dim.14), channel_id=1, replica_groups={{0,8,16,24},{1,9,17,25},{2,10,18,26},{3,11,19,27},{4,12,20,28},{5,13,21..., dimensions={0} | all-to-all | bytes 327680 | tf_op jit(solution)/shard_map/all_to_all | solution.py:567
  809.7 4.4 all-to-all-start.20
  820.4 11.0 %all-to-all-done.20.x_ref = bf16[8,4,160,128]{3,2,1,0:T(8,128)(2,1)} async-done(((bf16[8,4,160,128]{3,2,1,0:T(8,128)(2,1)}), bf16[8,4,160,128]{3,2,1,0:T(8,128)(2,1)}, u32[]{:S(2)}, u32[]{:S(2)}) %all-to-all-start.20) | async-done | bytes 1310752 | tf_op jit(solution)/shard_map/all_to_all | solution.py:567
  (84 shorter events, 53.6 us)
Async XLA Ops:
  4.5 7.6 copy-start.6
  4.5 7.8 copy-start.7
  4.5 8.5 %copy-start.5 = (f32[2,512]{1,0:T(2,128)S(1)}, f32[2,512]{1,0:T(2,128)}, u32[]{:S(2)}) copy-start(f32[2,512]{1,0:T(2,128)} %param.22) | copy-start | bytes 12292
  4.5 8.7 %copy-start.8 = (f32[2,2,128]{2,1,0:T(2,128)S(1)}, f32[2,2,128]{2,1,0:T(2,128)}, u32[]{:S(2)}) copy-start(f32[2,2,128]{2,1,0:T(2,128)} %param.20) | copy-start | bytes 6148
  4.5 8.9 %copy-start.9 = (f32[2,2,128]{2,1,0:T(2,128)S(1)}, f32[2,2,128]{2,1,0:T(2,128)}, u32[]{:S(2)}) copy-start(f32[2,2,128]{2,1,0:T(2,128)} %param.18) | copy-start | bytes 6148
  4.5 9.0 %copy-start.10 = (f32[2,128]{1,0:T(2,128)S(1)}, f32[2,128]{1,0:T(2,128)}, u32[]{:S(2)}) copy-start(f32[2,128]{1,0:T(2,128)} %param.24) | copy-start | bytes 3076
  4.5 48.7 %all-to-all-start.1 = ((bf16[16,32,16,128]{3,2,1,0:T(8,128)(2,1)}), bf16[16,32,16,128]{3,2,1,0:T(8,128)(2,1)}, u32[]{:S(2)}, u32[]{:S(2)}) async-start(bf16[16,32,16,128]{3,2,1,0:T(8,128)(2,1)} %bitcast.14), calls=%async_computation.1 | async-start | bytes 4194304 | tf_op jit(solution)/shard_map/all_to_all | solution.py:567
  12.0 2.6 copy-start.1
  12.1 3.6 copy-start.4
  12.3 4.2 copy-start.11
  54.5 11.8 %copy-start.3 = (bf16[2,512,128]{2,1,0:T(8,128)(2,1)S(1)}, bf16[2,512,128]{2,1,0:T(8,128)(2,1)}, u32[]{:S(2)}) copy-start(bf16[2,512,128]{2,1,0:T(8,128)(2,1)} %refs_19_.7) | copy-start | bytes 786436
  54.5 12.6 %copy-start.2 = (bf16[2,128,512]{2,1,0:T(8,128)(2,1)S(1)}, bf16[2,128,512]{2,1,0:T(8,128)(2,1)}, u32[]{:S(2)}) copy-start(bf16[2,128,512]{2,1,0:T(8,128)(2,1)} %refs_18_.7) | copy-start | bytes 786436
  54.5 52.5 %all-to-all-start.2 = ((bf16[16,32,16,128]{3,2,1,0:T(8,128)(2,1)}), bf16[16,32,16,128]{3,2,1,0:T(8,128)(2,1)S(1)}, u32[]{:S(2)}, u32[]{:S(2)}) async-start(bf16[16,32,16,128]{3,2,1,0:T(8,128)(2,1)} %bitcast.91), calls=%async_computation.2 | async-start | bytes 4194304 | tf_op jit(solution)/shard_map/all_to_all | solution.py:567
  65.8 2.1 collective-permute-start
  106.9 1.3 copy-start
  108.3 52.7 %all-to-all-start = ((bf16[16,32,16,128]{3,2,1,0:T(8,128)(2,1)}), bf16[16,32,16,128]{3,2,1,0:T(8,128)(2,1)}, u32[]{:S(2)}, u32[]{:S(2)}) async-start(bf16[16,32,16,128]{3,2,1,0:T(8,128)(2,1)} %bitcast.7), calls=%async_computation | async-start | bytes 4194304 | tf_op jit(solution)/shard_map/all_to_all | solution.py:567
  181.1 36.7 %all-to-all-start.4 = ((bf16[8,32,32,128]{3,2,1,0:T(8,128)(2,1)}), bf16[8,32,32,128]{3,2,1,0:T(8,128)(2,1)}, u32[]{:S(2)}, u32[]{:S(2)}) async-start(bf16[8,32,32,128]{3,2,1,0:T(8,128)(2,1)} %get-tuple-element.136), calls=%async_computation.4 | async-start | bytes 4194304 | tf_op jit(solution)/shard_map/all_to_all | solution.py:567
  217.8 30.1 %all-to-all-start.3 = ((bf16[8,32,32,128]{3,2,1,0:T(8,128)(2,1)}), bf16[8,32,32,128]{3,2,1,0:T(8,128)(2,1)}, u32[]{:S(2)}, u32[]{:S(2)}) async-start(bf16[8,32,32,128]{3,2,1,0:T(8,128)(2,1)} %get-tuple-element.135), calls=%async_computation.3 | async-start | bytes 4194304 | tf_op jit(solution)/shard_map/all_to_all | solution.py:567
  247.8 30.1 %all-to-all-start.6 = ((bf16[8,32,32,128]{3,2,1,0:T(8,128)(2,1)}), bf16[8,32,32,128]{3,2,1,0:T(8,128)(2,1)}, u32[]{:S(2)}, u32[]{:S(2)}) async-start(bf16[8,32,32,128]{3,2,1,0:T(8,128)(2,1)} %get-tuple-element.140), calls=%async_computation.6 | async-start | bytes 4194304 | tf_op jit(solution)/shard_map/all_to_all | solution.py:567
  277.9 36.2 %all-to-all-start.5 = ((bf16[8,32,32,128]{3,2,1,0:T(8,128)(2,1)}), bf16[8,32,32,128]{3,2,1,0:T(8,128)(2,1)}, u32[]{:S(2)}, u32[]{:S(2)}) async-start(bf16[8,32,32,128]{3,2,1,0:T(8,128)(2,1)} %get-tuple-element.138), calls=%async_computation.5 | async-start | bytes 4194304 | tf_op jit(solution)/shard_map/all_to_all | solution.py:567
  314.1 48.2 %all-to-all-start.8 = ((bf16[16,32,16,128]{3,2,1,0:T(8,128)(2,1)}), bf16[16,32,16,128]{3,2,1,0:T(8,128)(2,1)}, u32[]{:S(2)}, u32[]{:S(2)}) async-start(bf16[16,32,16,128]{3,2,1,0:T(8,128)(2,1)} %bitcast.84), calls=%async_computation.8 | async-start | bytes 4194304 | tf_op jit(solution)/shard_map/all_to_all | solution.py:567
  362.3 52.4 %all-to-all-start.7 = ((bf16[16,16,32,128]{3,2,1,0:T(8,128)(2,1)}), bf16[16,16,32,128]{3,2,1,0:T(8,128)(2,1)}, u32[]{:S(2)}, u32[]{:S(2)}) async-start(bf16[16,16,32,128]{3,2,1,0:T(8,128)(2,1)} %bitcast.94), calls=%async_computation.7 | async-start | bytes 4194304 | tf_op jit(solution)/shard_map/all_to_all | solution.py:567
  414.8 42.9 %all-to-all-start.10 = ((bf16[8,32,32,128]{3,2,1,0:T(8,128)(2,1)}), bf16[8,32,32,128]{3,2,1,0:T(8,128)(2,1)}, u32[]{:S(2)}, u32[]{:S(2)}) async-start(bf16[8,32,32,128]{3,2,1,0:T(8,128)(2,1)} %get-tuple-element.163), calls=%async_computation.10 | async-start | bytes 4194304 | tf_op jit(solution)/shard_map/all_to_all | solution.py:567
  457.7 34.3 %all-to-all-start.9 = ((bf16[8,32,32,128]{3,2,1,0:T(8,128)(2,1)}), bf16[8,32,32,128]{3,2,1,0:T(8,128)(2,1)}, u32[]{:S(2)}, u32[]{:S(2)}) async-start(bf16[8,32,32,128]{3,2,1,0:T(8,128)(2,1)} %get-tuple-element.154), calls=%async_computation.9 | async-start | bytes 4194304 | tf_op jit(solution)/shard_map/all_to_all | solution.py:567
  492.0 34.5 %all-to-all-start.13 = ((bf16[8,32,32,128]{3,2,1,0:T(8,128)(2,1)}), bf16[8,32,32,128]{3,2,1,0:T(8,128)(2,1)}, u32[]{:S(2)}, u32[]{:S(2)}) async-start(bf16[8,32,32,128]{3,2,1,0:T(8,128)(2,1)} %get-tuple-element.182), calls=%async_computation.13 | async-start | bytes 4194304 | tf_op jit(solution)/shard_map/all_to_all | solution.py:567
  526.5 30.3 %all-to-all-start.11 = ((bf16[8,32,32,128]{3,2,1,0:T(8,128)(2,1)}), bf16[8,32,32,128]{3,2,1,0:T(8,128)(2,1)}, u32[]{:S(2)}, u32[]{:S(2)}) async-start(bf16[8,32,32,128]{3,2,1,0:T(8,128)(2,1)} %get-tuple-element.172), calls=%async_computation.11 | async-start | bytes 4194304 | tf_op jit(solution)/shard_map/all_to_all | solution.py:567
  557.9 60.7 %all-to-all-start.12 = ((bf16[16,16,32,128]{3,2,1,0:T(8,128)(2,1)}), bf16[16,16,32,128]{3,2,1,0:T(8,128)(2,1)}, u32[]{:S(2)}, u32[]{:S(2)}) async-start(bf16[16,16,32,128]{3,2,1,0:T(8,128)(2,1)} %bitcast.90), calls=%async_computation.12 | async-start | bytes 4194304 | tf_op jit(solution)/shard_map/all_to_all | solution.py:567
  620.0 47.5 %all-to-all-start.14 = ((bf16[16,16,32,128]{3,2,1,0:T(8,128)(2,1)}), bf16[16,16,32,128]{3,2,1,0:T(8,128)(2,1)}, u32[]{:S(2)}, u32[]{:S(2)}) async-start(bf16[16,16,32,128]{3,2,1,0:T(8,128)(2,1)} %bitcast.89), calls=%async_computation.14 | async-start | bytes 4194304 | tf_op jit(solution)/shard_map/all_to_all | solution.py:567
  668.7 34.3 %all-to-all-start.15 = ((bf16[16,16,16,128]{3,2,1,0:T(8,128)(2,1)}), bf16[16,16,16,128]{3,2,1,0:T(8,128)(2,1)}, u32[]{:S(2)}, u32[]{:S(2)}) async-start(bf16[16,16,16,128]{3,2,1,0:T(8,128)(2,1)} %bitcast.96), calls=%async_computation.15 | async-start | bytes 2097152 | tf_op jit(solution)/shard_map/all_to_all | solution.py:567
  704.3 36.7 %all-to-all-start.16 = ((bf16[16,16,16,128]{3,2,1,0:T(8,128)(2,1)}), bf16[16,16,16,128]{3,2,1,0:T(8,128)(2,1)}, u32[]{:S(2)}, u32[]{:S(2)}) async-start(bf16[16,16,16,128]{3,2,1,0:T(8,128)(2,1)} %bitcast.97), calls=%async_computation.16 | async-start | bytes 2097152 | tf_op jit(solution)/shard_map/all_to_all | solution.py:567
  742.3 37.6 %all-to-all-start.17 = ((bf16[32,128,128]{2,1,0:T(8,128)(2,1)}), bf16[32,128,128]{2,1,0:T(8,128)(2,1)}, u32[]{:S(2)}, u32[]{:S(2)}) async-start(bf16[32,128,128]{2,1,0:T(8,128)(2,1)} %fusion.5), calls=%async_computation.17 | async-start | bytes 2097152 | tf_op jit(solution)/shard_map/all_to_all | solution.py:1026
  782.5 16.4 %all-to-all-start.18 = ((bf16[32,32,128]{2,1,0:T(8,128)(2,1)}), bf16[32,32,128]{2,1,0:T(8,128)(2,1)S(1)}, u32[]{:S(2)}, u32[]{:S(2)}) async-start(bf16[32,32,128]{2,1,0:T(8,128)(2,1)} %fusion.2), calls=%async_computation.18 | async-start | bytes 524288 | tf_op jit(solution)/shard_map/all_to_all | solution.py:1026
  809.7 21.7 %all-to-all-start.20 = ((bf16[8,4,160,128]{3,2,1,0:T(8,128)(2,1)}), bf16[8,4,160,128]{3,2,1,0:T(8,128)(2,1)}, u32[]{:S(2)}, u32[]{:S(2)}) async-start(bf16[8,4,160,128]{3,2,1,0:T(8,128)(2,1)} %broadcast_in_dim.15), calls=%async_computation.20 | async-start | bytes 2621440 | tf_op jit(solution)/shard_map/all_to_all | solution.py:567
